TPU v7x, 32 devices: a whole 2x2x4 slice. The times are simulated.
32 devices in a mesh: dom: 8 (over z, x), sub: 4 (over y, core).
Axes of the slice: x: 2, y: 2, z: 4, core: 2. Of those that a mesh axis runs over, the one named last changes fastest.
Arguments:
- positions: float32 [3, 262144], P(None, ('dom', 'sub')), may hold values from 0 to 1
- masses: float32 [262144], P(('dom', 'sub')), may hold values from 0.00029296876 to 0.0029296875
- cell_mass: float32 [4096], P(('dom', 'sub')), may hold values from 0.00234375 to 0.0234375
- cell_center: float32 [3, 4096], P(None, ('dom', 'sub')), may hold values from 0 to 1
- cell_quad: float32 [6, 4096], P(None, ('dom', 'sub')), may hold values from -0.0046875 to 0.0046875
- cell_list: int32 [4096, 128], P(('dom', 'sub')), may hold values from 0 to 4095
- leaf_list: int32 [4096, 16], P(('dom', 'sub')), may hold values from 0 to 575, as said below
- send_list: int32 [8, 4, 8, 8], P('dom', 'sub'), may hold values from 0 to 127
- send_count: int32 [8, 4, 8], P('dom', 'sub'), may hold values from 1 to 8, as said below
Outputs:
- accel: float32 [3, 262144], P(None, ('dom', 'sub'))
Inputs may be any that keep to these rules, and one draw needn't show every extreme that they name: `send_count`: counts fall off with the distance along the curve: an offset of one domain always carries 8 blocks, an offset of d domains at most max(1, 8 // d). `leaf_list`: each id names a block of the group's own domain or a slot of the far part that carries a block.
All inputs are finite; a program needn't handle non-finite values.
Results may differ from a plain program's by a relative error of at most 0.0003.
Values sent between devices are 32-bit elements; how exact they have to be, the bound alone decides.
No kernel may reach another device: no remote copies, remote signals or barrier semaphores. Data moves between devices by JAX's collectives and lax.ppermute only.
A program may use at most 128 MiB of HBM per device.

v0:
```python
import functools

import jax
import jax.numpy as jnp
from jax import lax
from jax.experimental import pallas as pl
from jax.experimental.pallas import tpu as pltpu
from jax.sharding import PartitionSpec as P

LEAF = 64
LEAF_DEV = 128
NCELL = 128
NLEAF = 16
RANGE = 4
CAP = 8
PAIRS = LEAF_DEV // 2
OUT_UNITS = CAP // 2
OWN_ROWS = 4 * PAIRS
OUT_ROWS = 4 * OUT_UNITS
CELL_COMPS = 10
CELL_PAD = 16
SENT_ROWS = OUT_ROWS + CELL_PAD
OFFSETS = list(range(-RANGE, 0)) + list(range(1, RANGE + 1))

softening_sq = 0.0025
GRID_ROUND = 49152.0
F32 = jnp.float32
BF16 = jnp.bfloat16

H_ROWS = 32
Q_ROWS = 64
V_ROWS = 16
U_ROWS = 48
Q_AT = H_ROWS
V_AT = Q_AT + Q_ROWS
U_AT = V_AT + V_ROWS
CELL_ROWS = U_AT + U_ROWS
M_ROWS = 8


def rounded(value):
    return value.astype(BF16).astype(F32)


def three_parts(value):
    first = rounded(value)
    rest = value - first
    second = rounded(rest)
    return first, second, rest - second


def two_parts(value):
    first = value.astype(BF16)
    return first, (value - first.astype(F32)).astype(BF16)


def grid_parts(value):
    high = (value + GRID_ROUND) - GRID_ROUND
    low = value - high
    first = rounded(low)
    return high, low, first, low - first


def norm_parts(parts, extra=None):
    big = sum(high * high for high, _, _, _ in parts)
    small = sum(low * (2.0 * high + low) for high, low, _, _ in parts)
    if extra is not None:
        small = small + extra
    return three_parts(big), three_parts(small)


def put_own(pos_ref, mass_ref, own_ref):
    for pair in range(PAIRS):
        lanes = pl.ds(128 * pair, 128)
        own_ref[4 * pair : 4 * pair + 3, :] = pos_ref[:, lanes]
        own_ref[4 * pair + 3 : 4 * pair + 4, :] = mass_ref[:, lanes]


def pack_kernel(n_dom, *refs):
    ins, outs, scratch, (out_ref, sent_ref, sems) = refs[:9], refs[9:12], refs[12:21], refs[21:]
    results = [
        pltpu.make_async_copy(out_ref.at[pl.ds(0, OWN_ROWS)], outs[0], sems.at[9]),
        pltpu.make_async_copy(sent_ref.at[pl.ds(0, n_dom)], outs[1], sems.at[10]),
        pltpu.make_async_copy(out_ref, outs[2], sems.at[11]),
    ]
    copies = [pltpu.make_async_copy(src, dst, sems.at[at]) for at, (src, dst) in enumerate(zip(ins, scratch))]
    for copy in copies:
        copy.start()
    pos_ref, mass_ref, cmass_ref, center_ref, quad_ref, cl_ref, ll_ref, list_ref, count_ref = scratch
    me = lax.axis_index("dom")
    left = lax.broadcasted_iota(jnp.int32, (4, 128), 1) < LEAF
    sent_ref[...] = jnp.zeros((n_dom + 1, SENT_ROWS, 128), F32)
    for copy in copies:
        copy.wait()
    put_own(pos_ref, mass_ref, out_ref)
    out_ref[OWN_ROWS : OWN_ROWS + LEAF_DEV, :] = cl_ref[...].astype(F32)
    out_ref[OWN_ROWS + LEAF_DEV :, :] = ll_ref[...].astype(F32)

    def put_cells(target, carry):
        sent_ref[target, OUT_ROWS : OUT_ROWS + 1, :] = cmass_ref[...]
        sent_ref[target, OUT_ROWS + 1 : OUT_ROWS + 4, :] = center_ref[...]
        sent_ref[target, OUT_ROWS + 4 : OUT_ROWS + 10, :] = quad_ref[...]
        return carry

    lax.fori_loop(0, n_dom, put_cells, 0)

    def half(slot, j, right):
        block = list_ref[slot, j]
        value = out_ref[pl.ds(pl.multiple_of(4 * (block // 2), 4), 4), :]
        value = jnp.where(j < count_ref[0, slot], value, 0.0)
        return jnp.where((block & 1) == right, value, pltpu.roll(value, LEAF, 1))

    for slot in range(2 * RANGE):
        target = me + OFFSETS[slot]
        target = jnp.where((target >= 0) & (target < n_dom), target, n_dom)
        for unit in range(OUT_UNITS):
            sent_ref[target, 4 * unit : 4 * unit + 4, :] = jnp.where(left, half(slot, 2 * unit, 0), half(slot, 2 * unit + 1, 1))
    for copy in results:
        copy.start()
    for copy in results:
        copy.wait()


def target_h_rows(parts, one, zero):
    big, small = norm_parts(parts, softening_sq)
    minus_high = [-2.0 * part[0] for part in parts]
    minus_one = [-2.0 * part[2] for part in parts]
    minus_two = [-2.0 * part[3] for part in parts]
    rows = minus_high + [one] * 3 + list(big) + minus_high + minus_one + minus_high
    return rows + minus_two + minus_one + [one] * 3 + list(small) + [zero] * 2


def target_features(octet, tg_ref, ce_ref, feat_ref, ah_ref):
    left = lax.broadcasted_iota(jnp.int32, (8, 128), 1) < LEAF
    one = jnp.ones((8, 128), F32)
    zero = jnp.zeros((8, 128), F32)
    parts, centred = [], []
    for comp in range(3):
        rows = pl.ds(octet * 32 + comp, 8, stride=4)
        value = tg_ref[rows, :]
        first = jnp.broadcast_to(value[:, 0:1], (8, 128))
        second = jnp.broadcast_to(value[:, LEAF : LEAF + 1], (8, 128))
        ce_ref[comp, pl.ds(octet * 16, 8, stride=2), :] = first
        ce_ref[comp, pl.ds(octet * 16 + 1, 8, stride=2), :] = second
        value = value - jnp.where(left, first, second)
        tg_ref[rows, :] = value
        centred.append(value)
        parts.append(grid_parts(value))
    rows = target_h_rows(parts, one, zero)
    x, y, z = centred
    split = [three_parts(v) for v in (x, y, z, x * x, y * y, z * z, x * y, x * z, y * z)]
    for which in (0, 0, 1, 0, 1, 2):
        rows += [part[which] for part in split]
    rows += [one] * 3 + [zero] * 7
    for at, value in enumerate(rows):
        feat_ref[8 * at : 8 * at + 8, :] = value
    for sub in range(8):
        features = feat_ref[pl.ds(sub, H_ROWS + Q_ROWS, stride=8), :].T.astype(BF16)
        ah_ref[octet * 8 + sub, :, 0 : H_ROWS + Q_ROWS] = features


def source_h_rows(parts):
    (p1, p2, p3), (s1, s2, s3) = norm_parts(parts)
    high = [part[0] for part in parts]
    one = [part[2] for part in parts]
    two = [part[3] for part in parts]
    rows = dict(enumerate(high + [p1, p2, p3]))
    rows.update(enumerate(one + high + two + high + one + [s1, s2, s3], 9))
    return rows


def put_rows(ref, rows):
    for at, value in rows.items():
        ref[8 * at : 8 * at + 8, :] = value


def fill_constant_rows(ref, count):
    one = jnp.ones((8, 128), F32)
    zero = jnp.zeros((8, 128), F32)
    for at in range(count):
        ones = at in (6, 7, 8, 27, 28, 29) or at == V_AT + 3
        ref[8 * at : 8 * at + 8, :] = one if ones else zero


def cell_features(n_dom, n_sub, octet, cl_ref, spread_ref, ce_ref, cf_ref, cm_ref):
    ids = cl_ref[pl.ds(pl.multiple_of(8 * octet, 8), 8), :]
    lane = ids & 127
    owner = ids >> 7
    me = lax.axis_index("sub")

    def look_up(dom, shift, found):
        here = owner == dom * n_sub + lax.rem(me + n_sub - shift, n_sub)
        new = []
        for comp in range(CELL_COMPS):
            value = jnp.take_along_axis(spread_ref[dom, shift, comp], lane, axis=1, mode="promise_in_bounds")
            new.append(jnp.where(here, value, found[comp]))
        return tuple(new)

    found = tuple(jnp.zeros((8, 128), F32) for _ in range(CELL_COMPS))
    if n_dom <= 8:
        for dom in range(n_dom):
            for shift in range(n_sub):
                found = look_up(dom, shift, found)
                yield
    else:

        def one_domain(dom, found):
            for shift in range(n_sub):
                found = look_up(dom, shift, found)
            return found

        found = lax.fori_loop(0, n_dom, one_domain, found)
    mass, cx, cy, cz, xx, yy, zz, xy, xz, yz = found
    yield "found"
    cm_ref[...] = mass
    rows8 = pl.ds(pl.multiple_of(8 * octet, 8), 8)
    cx, cy, cz = [value - ce_ref[comp, rows8, :] for comp, value in enumerate((cx, cy, cz))]
    put_rows(cf_ref, source_h_rows([grid_parts(value) for value in (cx, cy, cz)]))
    yield
    qx = xx * cx + xy * cy + xz * cz
    qy = xy * cx + yy * cy + yz * cz
    qz = xz * cx + yz * cy + zz * cz
    const = three_parts(2.5 * (qx * cx + qy * cy + qz * cz))
    linear = [-5.0 * qx, -5.0 * qy, -5.0 * qz]
    square = [2.5 * xx, 2.5 * yy, 2.5 * zz, 5.0 * xy, 5.0 * xz, 5.0 * yz]
    split = [three_parts(value) for value in linear + square]
    rows = []
    for which in (0, 1, 0, 2, 1, 0):
        rows += [part[which] for part in split]
    rows += list(const)
    put_rows(cf_ref, dict(enumerate(rows, Q_AT)))
    yield
    for comp, value in enumerate((cx, cy, cz)):
        for which, part in enumerate(three_parts(value)):
            cf_ref[8 * (V_AT + 4 * which + comp) : 8 * (V_AT + 4 * which + comp) + 8, :] = part
    yield
    columns = {name: three_parts(value) for name, value in dict(xx=xx, yy=yy, zz=zz, xy=xy, xz=xz, yz=yz, cx=qx, cy=qy, cz=qz).items()}
    order = (("xx", "xy", "xz"), ("xy", "yy", "yz"), ("xz", "yz", "zz"), ("cx", "cy", "cz"))
    for which in range(3):
        for column, names in enumerate(order):
            for row, name in enumerate(names):
                at = U_AT + 16 * which + 4 * column + row
                cf_ref[8 * at : 8 * at + 8, :] = columns[name][which]


def source_moments(group, ll_ref, tab_ref, ce_ref, raw_ref, sf_ref):
    left = lax.broadcasted_iota(jnp.int32, (4, 128), 1) < LEAF
    for pair in range(NLEAF // 2):
        first = tab_ref[ll_ref[2 * pair, group]]
        second = tab_ref[ll_ref[2 * pair + 1, group]]
        raw_ref[4 * pair : 4 * pair + 4, :] = jnp.where(left, first, second)
    value = [raw_ref[pl.ds(comp, 8, stride=4), :] for comp in range(4)]
    mass = value[3]
    centred = [value[comp] - ce_ref[comp, pl.ds(group, 1), :] for comp in range(3)]
    for comp, v in enumerate([mass * v for v in centred] + [mass]):
        high = rounded(v)
        for which, part in enumerate((high, v - high)):
            at = 4 * which + comp
            sf_ref[8 * at : 8 * at + 8, :] = part


def transposed_dot(rows, weights):
    return lax.dot_general(rows, weights, (((1,), (1,)), ((), ())), preferred_element_type=F32)


def stacked(value):
    return jnp.concatenate(two_parts(value), axis=0)


def cell_group(sub, target, cf_ref, cm_ref):
    def cell_rows(at, count):
        return cf_ref[pl.ds(8 * at + sub, count, stride=8), :].astype(BF16)

    forms = jnp.concatenate(
        [
            jnp.concatenate([cell_rows(0, H_ROWS), jnp.zeros((H_ROWS, 128), BF16)], axis=1),
            jnp.concatenate([jnp.zeros((Q_ROWS, 128), BF16), cell_rows(Q_AT, Q_ROWS)], axis=1),
        ],
        axis=0,
    )
    forms = jnp.dot(target[:, 0 : H_ROWS + Q_ROWS], forms, preferred_element_type=F32)
    dist_sq, quad_form = forms[:, 0:128], forms[:, 128:256]
    inv = lax.rsqrt(dist_sq)
    inv_two = inv * inv
    inv_three = inv * inv_two
    pull = inv_three * (cm_ref[pl.ds(sub, 1), :] + quad_form * (inv_two * inv_two))
    moments = jnp.concatenate(
        [
            jnp.concatenate([cell_rows(V_AT, V_ROWS), jnp.zeros((V_ROWS, 128), BF16)], axis=1),
            jnp.concatenate([jnp.zeros((U_ROWS, 128), BF16), cell_rows(U_AT, U_ROWS)], axis=1),
        ],
        axis=0,
    )
    both = jnp.concatenate([stacked(pull), stacked(inv_three * inv_two)], axis=1)
    return both, moments


def pair_lanes(pair):
    return pl.ds(pl.multiple_of(128 * pair, 128), 128)


def pair_place(tg_ref, pair):
    return tg_ref[pl.ds(pl.multiple_of(4 * pair, 4), 4), :]


def point_sums(sums, place):
    sums = sums + pltpu.roll(sums, 4, 0)
    return sums[0:3] - place[0:3] * sums[3:4]


def cell_pull(octet, tg_ref, ah_ref, cf_ref, cm_ref, out_ref):
    upper = lax.broadcasted_iota(jnp.int32, (8, 128), 0) < 4
    left = lax.broadcasted_iota(jnp.int32, (LEAF, 128), 1) < LEAF
    for inner in range(4):
        pair = octet * 4 + inner
        first, first_moments = cell_group(2 * inner, ah_ref[pair, 0:LEAF, :], cf_ref, cm_ref)
        yield
        second, second_moments = cell_group(2 * inner + 1, ah_ref[pair, LEAF:, :], cf_ref, cm_ref)
        moments = jnp.concatenate([first_moments, second_moments], axis=0)
        sums = transposed_dot(jnp.concatenate([first, second], axis=0), moments)
        yield
        sums = jnp.where(left, sums[0:64] + sums[64:128], sums[128:192] + sums[192:256]).T
        sums = jnp.concatenate([sums[0:64], sums[64:128]], axis=1)
        place = pair_place(tg_ref, pair)
        x, y, z = [place[comp : comp + 1, :] for comp in range(3)]
        quads = sums[16:32] + sums[32:48] + sums[48:64]
        turned = quads[0:8] * jnp.where(upper, x, y) + quads[8:16] * jnp.where(upper, z, -1.0)
        turned = turned + pltpu.roll(turned, 4, 0)
        out_ref[:, pair_lanes(pair)] = point_sums(sums[0:8] + sums[8:16], place) + turned[0:3]


def put_block_pair(tab_ref, block, value):
    left = lax.broadcasted_iota(jnp.int32, (4, 128), 1) < LEAF
    turned = pltpu.roll(value, LEAF, 1)
    tab_ref[block] = jnp.where(left, value, turned)
    tab_ref[block + 1] = jnp.where(left, turned, value)


def put_eight_pairs(rows_ref, block, coords, feat_ref):
    put_rows(feat_ref, source_h_rows([grid_parts(value) for value in coords]))
    for pair in range(8):
        columns = feat_ref[pl.ds(pair, H_ROWS, stride=8), :].astype(BF16)
        spread = jnp.concatenate([columns] * 4, axis=0).T
        rows_ref[block + 2 * pair] = spread[0:LEAF]
        rows_ref[block + 2 * pair + 1] = spread[LEAF:]


def prepare_kernel(n_dom, n_sub, *refs):
    bundle_ref, near_refs, recv_ref = refs[0], refs[1:n_sub], refs[n_sub]
    tab_ref, rows_ref, at_ref, tg_ref, ce_ref, ah_ref, cl_ref, ll_ref, feat_ref, four_ref = refs[n_sub + 1 :]
    own_ref = bundle_ref.at[0:OWN_ROWS]
    cl_ref[...] = bundle_ref[OWN_ROWS : OWN_ROWS + LEAF_DEV, :].astype(jnp.int32)
    ll_ref[...] = bundle_ref[OWN_ROWS + LEAF_DEV :, :].astype(jnp.int32)
    for at in range(8):
        fill_constant_rows(four_ref.at[at], H_ROWS)
    me = lax.axis_index("sub")

    def near_blocks(shift, near_ref):
        seg = lax.rem(me + n_sub - shift, n_sub)

        def near(step, carry):
            for at in range(8):
                octet = 8 * step + at
                block = seg * LEAF_DEV + 16 * octet
                first = pl.multiple_of(32 * octet, 32)
                for pair in range(8):
                    put_block_pair(tab_ref, block + 2 * pair, near_ref[pl.ds(pl.multiple_of(first + 4 * pair, 4), 4), :])
                coords = [near_ref[pl.ds(first + comp, 8, stride=4), :] for comp in range(3)]
                put_eight_pairs(rows_ref, block, coords, four_ref.at[at])
            return carry

        lax.fori_loop(0, PAIRS // 64, near, 0)

    for shift in range(1, n_sub):
        near_blocks(shift, near_refs[shift - 1])
    far_tables(n_dom, n_sub * LEAF_DEV, recv_ref, tab_ref, rows_ref, four_ref)
    near_blocks(0, own_ref)
    tg_ref[...] = own_ref[...]

    def targets(step, carry):
        for at in range(2):
            octet = 2 * step + at
            target_features(octet, tg_ref, ce_ref, feat_ref.at[at], ah_ref)
            target_rows(octet, own_ref, four_ref.at[at], at_ref)
        return carry

    lax.fori_loop(0, PAIRS // 16, targets, 0)


def far_tables(n_dom, first_block, recv_ref, tab_ref, rows_ref, four_ref):
    me = lax.axis_index("dom")
    for two in range(RANGE):
        halves = []
        for slot in (2 * two, 2 * two + 1):
            source = me - OFFSETS[slot]
            inside = (source >= 0) & (source < n_dom)
            source = jnp.clip(source, 0, n_dom - 1)
            for unit in range(OUT_UNITS):
                value = jnp.where(inside, recv_ref[source, 4 * unit : 4 * unit + 4, :], 0.0)
                put_block_pair(tab_ref, first_block + slot * CAP + 2 * unit, value)
            halves.append([jnp.where(inside, recv_ref[source, pl.ds(comp, OUT_UNITS, stride=4), :], 0.0) for comp in range(3)])
        coords = [jnp.concatenate([one, other], axis=0) for one, other in zip(*halves)]
        put_eight_pairs(rows_ref, first_block + 2 * two * CAP, coords, four_ref.at[two])


def target_rows(octet, own_ref, feat_ref, at_ref):
    one = jnp.ones((8, 128), F32)
    zero = jnp.zeros((8, 128), F32)
    parts = [grid_parts(own_ref[pl.ds(octet * 32 + comp, 8, stride=4), :]) for comp in range(3)]
    for at, value in enumerate(target_h_rows(parts, one, zero)):
        feat_ref[8 * at : 8 * at + 8, :] = value
    for pair in range(8):
        at_ref[octet * 8 + pair] = feat_ref[pl.ds(pair, H_ROWS, stride=8), :].astype(BF16)


def run(strand, steps=None):
    taken = 0
    while steps is None or taken < steps:
        taken += 1
        if next(strand, "end") == "end":
            return


def pull_kernel(n_dom, n_sub, *refs):
    cell_refs = refs[:n_sub]
    tab_ref, rows_ref, at_ref, tg_ref, ce_ref, ah_ref, cl_ref, ll_in, out_ref = refs[n_sub : n_sub + 9]
    ll_ref, spread_ref, cf_ref, cm_ref, raw_ref, even_ref, odd_ref, dist_even, dist_odd, sem = refs[n_sub + 9 :]
    copy = pltpu.make_async_copy(ll_in, ll_ref, sem)
    copy.start()
    fill_constant_rows(cf_ref, CELL_ROWS)

    def build(octet):
        return cell_features(n_dom, n_sub, octet, cl_ref, spread_ref, ce_ref, cf_ref, cm_ref)

    def spread(dom, carry):
        for shift in range(n_sub):
            for comp in range(CELL_COMPS):
                row = cell_refs[shift][dom, comp : comp + 1, :]
                spread_ref[dom, shift, comp] = jnp.broadcast_to(row, (8, 128))
        return carry

    lax.fori_loop(0, n_dom, spread, 0)

    run(build(0))
    copy.wait()
    left = lax.broadcasted_iota(jnp.int32, (M_ROWS, 128), 1) < LEAF
    left_target = lax.broadcasted_iota(jnp.int32, (H_ROWS, 128), 1) < LEAF
    owner = (lax.broadcasted_iota(jnp.int32, (LEAF, 128), 1) // H_ROWS).astype(BF16)
    lower_half, first_own, third_own = owner < 2.0, owner == 0.0, owner == 2.0

    def features(quad, raw_at, slot_ref):
        for group in range(4):
            source_moments(4 * quad + group, ll_ref, tab_ref, ce_ref, raw_ref.at[raw_at + group], slot_ref.at[group])
            yield

    def distances(quad, dist_ref):
        nothing = jnp.zeros((H_ROWS, 128), BF16)
        first, second = at_ref[2 * quad], at_ref[2 * quad + 1]
        targets = jnp.concatenate(
            [
                jnp.concatenate([jnp.where(left_target, first, nothing), nothing], axis=1),
                jnp.concatenate([jnp.where(left_target, nothing, first), nothing], axis=1),
                jnp.concatenate([nothing, jnp.where(left_target, second, nothing)], axis=1),
                jnp.concatenate([nothing, jnp.where(left_target, nothing, second)], axis=1),
            ],
            axis=0,
        )
        sources = []
        for j in range(NLEAF):
            rows = [rows_ref[ll_ref[j, 4 * quad + group]] for group in range(4)]
            low = jnp.where(first_own, rows[0], rows[1])
            high = jnp.where(third_own, rows[2], rows[3])
            sources.append(jnp.where(lower_half, low, high))
            if j % 8 == 7:
                rows = pl.ds(LEAF * (j - 7), 8 * LEAF)
                dist_ref[rows, :] = jnp.dot(jnp.concatenate(sources, axis=0), targets, preferred_element_type=F32)
                sources = []
                yield

    def pull(quad, slot_ref, dist_ref):
        total = jnp.zeros((4 * M_ROWS, 256), F32)
        for chunk in range(8):
            inv = lax.rsqrt(dist_ref[128 * chunk : 128 * chunk + 128, :])
            weights = stacked(inv * inv * inv)
            rows = [slot_ref[group, pl.ds(chunk, M_ROWS, stride=8), :] for group in range(4)]
            rows = jnp.concatenate(rows, axis=0).astype(BF16)
            total += jnp.dot(jnp.concatenate([rows, rows], axis=1), weights, preferred_element_type=F32)
            yield
        for side in range(2):
            pair = 2 * quad + side
            at, columns = 2 * M_ROWS * side, slice(128 * side, 128 * side + 128)
            sums = jnp.where(left, total[at : at + M_ROWS, columns], total[at + M_ROWS : at + 2 * M_ROWS, columns])
            lanes = pair_lanes(pair)
            out_ref[:, lanes] = out_ref[:, lanes] + point_sums(sums, pair_place(tg_ref, pair))

    quads, octets = LEAF_DEV // 4, LEAF_DEV // 8
    run(features(0, 0, even_ref))
    run(distances(0, dist_even))

    def one_octet(octet, carry):
        quad = 2 * octet
        after = jnp.minimum(quad + 2, quads - 1)
        cells = cell_pull(octet, tg_ref, ah_ref, cf_ref, cm_ref, out_ref)
        coming = build(jnp.minimum(octet + 1, octets - 1))
        for half, (now, slot_ref, dist_ref, ahead, ahead_slot, ahead_dist, raw_at) in enumerate(
            (
                (quad, even_ref, dist_even, quad + 1, odd_ref, dist_odd, 4),
                (quad + 1, odd_ref, dist_odd, after, even_ref, dist_even, 0),
            )
        ):
            direct = pull(now, slot_ref, dist_ref)
            moments, distance = features(ahead, raw_at, ahead_slot), distances(ahead, ahead_dist)
            for step in range(8):
                if step in (1, 4):
                    run(distance, 1)
                run(direct, 1)
                if step % 2 == 0:
                    run(moments, 1)
                if half == 0 or step < 4:
                    run(coming, 3)
                    if step % 4 != 3:
                        run(cells, 1)
                elif step == 4:
                    run(cells)
                else:
                    run(coming, 1)
            run(moments)
            run(distance)
            run(direct)
        run(coming)
        return carry

    lax.fori_loop(0, octets, one_octet, 0)


def on_device(n_dom, n_sub, positions, masses, cell_mass, cell_center, cell_quad, cell_list, leaf_list, send_list, send_count):
    vmem = pl.BlockSpec(memory_space=pltpu.VMEM)
    smem = pl.BlockSpec(memory_space=pltpu.SMEM)
    anywhere = pl.BlockSpec(memory_space=pl.ANY)

    def limit(mib):
        return pltpu.CompilerParams(vmem_limit_bytes=mib * 1024 * 1024)

    ins = (
        positions,
        masses.reshape(1, -1),
        cell_mass.reshape(1, -1),
        cell_center,
        cell_quad,
        cell_list,
        leaf_list.T,
        send_list.reshape(2 * RANGE, CAP),
        send_count.reshape(1, 2 * RANGE),
    )
    bundle_rows = OWN_ROWS + LEAF_DEV + NLEAF
    packed, sent, bundle = pl.pallas_call(
        functools.partial(pack_kernel, n_dom),
        out_shape=(
            jax.ShapeDtypeStruct((OWN_ROWS, 128), F32),
            jax.ShapeDtypeStruct((n_dom, SENT_ROWS, 128), F32),
            jax.ShapeDtypeStruct((bundle_rows, 128), F32),
        ),
        in_specs=[pl.BlockSpec(memory_space=pltpu.HBM)] * 9,
        out_specs=[anywhere] * 3,
        scratch_shapes=[pltpu.VMEM(array.shape, array.dtype) for array in ins[:7]]
        + [pltpu.SMEM(array.shape, jnp.int32) for array in ins[7:]]
        + [
            pltpu.VMEM((bundle_rows, 128), F32),
            pltpu.VMEM((n_dom + 1, SENT_ROWS, 128), F32),
            pltpu.SemaphoreType.DMA((12,)),
        ],
        compiler_params=limit(63),
        name="pack_own",
    )(*ins)
    received = lax.all_to_all(sent, "dom", split_axis=0, concat_axis=0, tiled=True)

    def around(value):
        pieces = [value]
        for shift in range(1, n_sub):
            pieces.append(lax.ppermute(value, "sub", [(seg, (seg + shift) % n_sub) for seg in range(n_sub)]))
        return pieces

    nearby = around(packed)
    cells = around(received[:, OUT_ROWS:])
    n_blocks = n_sub * LEAF_DEV + 2 * RANGE * CAP
    prepared = pl.pallas_call(
        functools.partial(prepare_kernel, n_dom, n_sub),
        out_shape=(
            jax.ShapeDtypeStruct((n_blocks, 4, 128), F32),
            jax.ShapeDtypeStruct((n_blocks, LEAF, 128), BF16),
            jax.ShapeDtypeStruct((PAIRS, H_ROWS, 128), BF16),
            jax.ShapeDtypeStruct((OWN_ROWS, 128), F32),
            jax.ShapeDtypeStruct((3, LEAF_DEV, 128), F32),
            jax.ShapeDtypeStruct((PAIRS, 128, 128), BF16),
            jax.ShapeDtypeStruct((LEAF_DEV, NCELL), jnp.int32),
            jax.ShapeDtypeStruct((NLEAF, LEAF_DEV), jnp.int32),
        ),
        in_specs=[vmem] * (n_sub + 1),
        out_specs=[vmem] * 8,
        scratch_shapes=[
            pltpu.VMEM((2, 8 * (H_ROWS + Q_ROWS), 128), F32),
            pltpu.VMEM((8, 8 * H_ROWS, 128), F32),
        ],
        compiler_params=limit(24),
        cost_estimate=pl.CostEstimate(flops=0, bytes_accessed=20_000_000, transcendentals=0),
        name="prepare",
    )(bundle, *nearby[1:], received)
    return pl.pallas_call(
        functools.partial(pull_kernel, n_dom, n_sub),
        out_shape=jax.ShapeDtypeStruct((3, LEAF_DEV * LEAF), F32),
        in_specs=[vmem] * (n_sub + 8),
        out_specs=vmem,
        scratch_shapes=[
            pltpu.SMEM((NLEAF, LEAF_DEV), jnp.int32),
            pltpu.VMEM((n_dom, n_sub, CELL_COMPS, 8, 128), F32),
            pltpu.VMEM((8 * CELL_ROWS, 128), F32),
            pltpu.VMEM((8, 128), F32),
            pltpu.VMEM((8, 32, 128), F32),
            pltpu.VMEM((4, 8 * M_ROWS, 128), F32),
            pltpu.VMEM((4, 8 * M_ROWS, 128), F32),
            pltpu.VMEM((NLEAF * LEAF, 256), F32),
            pltpu.VMEM((NLEAF * LEAF, 256), F32),
            pltpu.SemaphoreType.DMA(()),
        ],
        compiler_params=limit(24),
        name="pull",
    )(*cells, *prepared)


def solution(mesh):
    sharded = P(("dom", "sub"))
    return jax.shard_map(
        functools.partial(on_device, mesh.shape["dom"], mesh.shape["sub"]),
        mesh=mesh,
        in_specs=(
            P(None, ("dom", "sub")),
            sharded,
            sharded,
            P(None, ("dom", "sub")),
            P(None, ("dom", "sub")),
            P(("dom", "sub"), None),
            P(("dom", "sub"), None),
            P("dom", "sub", None, None),
            P("dom", "sub", None),
        ),
        out_specs=P(None, ("dom", "sub")),
        check_vma=False,
    )
```

profile of v0, /device:TPU:0, one launch (start us, length us, event | category | flops | bytes accessed | tf_op | source)
XLA Modules:
  0.0 48.0 jit_solution(3138679674947803544)
XLA Ops:
  0.0 2.4 %pack_own.1 = (f32[256,128]{1,0:T(8,128)}, f32[8,32,128]{2,1,0:T(8,128)}, f32[400,128]{1,0:T(8,128)}) custom-call(f32[3,8192]{1,0:T(4,128)} %refs_0_.1, f32[1,8192]{1,0:T(1,128)} %bitcast.5, f32[1,128]{1,0:T(1,128)} %bitcast.8, f32[3,128]{1,0:T(4,128)} %refs_3_.1, f32[6,128]{1,0:T(8,128)} %refs_4_.1, s32[128,128]{1,0:T(8,128)} %refs_5_.1, ...), custom_call_target="tpu_custom_call" | custom-call | tf_op jit(solution)/shard_map/pack_own/pallas_call | solution.py:556
  2.4 7.3 %all-to-all-start = ((f32[8,32,128]{2,1,0:T(8,128)}), f32[8,32,128]{2,1,0:T(8,128)S(1)}, u32[]{:S(2)}, u32[]{:S(2)}) async-start(f32[8,32,128]{2,1,0:T(8,128)} %get-tuple-element.16), calls=%async_computation | async-start | bytes 262144 | tf_op jit(solution)/shard_map/all_to_all | solution.py:575
  9.7 0.0 collective-permute-start.3
  9.7 1.6 %collective-permute-start.4 = (f32[256,128]{1,0:T(8,128)}, f32[256,128]{1,0:T(8,128)S(1)}, u32[]{:S(2)}, u32[]{:S(2)}) collective-permute-start(f32[256,128]{1,0:T(8,128)} %get-tuple-element.18), channel_id=1, source_target_pairs={{0,2},{1,3},{2,0},{3,1},{4,6},{5,7},{6,4},{7,5},{8,10},{9,11},{10,... | collective-permute-start | bytes 393224 | tf_op jit(solution)/shard_map/ppermute | solution.py:580
  11.3 1.4 %collective-permute-start.5 = (f32[256,128]{1,0:T(8,128)}, f32[256,128]{1,0:T(8,128)S(1)}, u32[]{:S(2)}, u32[]{:S(2)}) collective-permute-start(f32[256,128]{1,0:T(8,128)} %get-tuple-element.18), channel_id=1, source_target_pairs={{0,3},{1,0},{2,1},{3,2},{4,7},{5,4},{6,5},{7,6},{8,11},{9,8},{10,9... | collective-permute-start | bytes 393224 | tf_op jit(solution)/shard_map/ppermute | solution.py:580
  12.7 4.4 %all-to-all-done.refs_4_ = f32[8,32,128]{2,1,0:T(8,128)S(1)} async-done(((f32[8,32,128]{2,1,0:T(8,128)}), f32[8,32,128]{2,1,0:T(8,128)S(1)}, u32[]{:S(2)}, u32[]{:S(2)}) %all-to-all-start) | async-done | bytes 131104 | tf_op jit(solution)/shard_map/all_to_all | solution.py:575
  17.0 0.0 collective-permute-start
  17.0 1.6 %collective-permute-start.1 = (f32[8,16,128]{2,1,0:T(8,128)S(1)}, f32[8,16,128]{2,1,0:T(8,128)S(1)}, u32[]{:S(2)}, u32[]{:S(2)}) collective-permute-start(f32[8,16,128]{2,1,0:T(8,128)S(1)} %slice.4.refs_0_), channel_id=1, source_target_pairs={{0,2},{1,3},{2,0},{3,1},{4,6},{5,7},{6,4},{7,5},{8,10},{9,11},{10,... | collective-permute-start | bytes 196616 | tf_op jit(solution)/shard_map/ppermute | solution.py:580
  18.6 0.0 collective-permute-done.3.refs_1_
  18.6 1.4 %collective-permute-start.2 = (f32[8,16,128]{2,1,0:T(8,128)S(1)}, f32[8,16,128]{2,1,0:T(8,128)S(1)}, u32[]{:S(2)}, u32[]{:S(2)}) collective-permute-start(f32[8,16,128]{2,1,0:T(8,128)S(1)} %slice.4.refs_0_), channel_id=1, source_target_pairs={{0,3},{1,0},{2,1},{3,2},{4,7},{5,4},{6,5},{7,6},{8,11},{9,8},{10,9... | collective-permute-start | bytes 196616 | tf_op jit(solution)/shard_map/ppermute | solution.py:580
  20.0 0.0 collective-permute-done.4.refs_2_
  20.0 0.0 collective-permute-done.5.refs_3_
  20.0 0.0 copy-start
  20.0 0.9 %copy-done = f32[400,128]{1,0:T(8,128)S(1)} copy-done((f32[400,128]{1,0:T(8,128)S(1)}, f32[400,128]{1,0:T(8,128)}, u32[]{:S(2)}) %copy-start) | copy-done | bytes 204824
  21.0 4.2 %prepare.1 = (f32[576,4,128]{2,1,0:T(4,128)S(1)}, bf16[576,64,128]{2,1,0:T(8,128)(2,1)S(1)}, bf16[64,32,128]{2,1,0:T(8,128)(2,1)S(1)}, f32[256,128]{1,0:T(8,128)...) custom-call(f32[400,128]{1,0:T(8,128)S(1)} %copy-done, ...), custom_call_target="tpu_custom_call" | custom-call | bytes 20000000 | tf_op jit(solution)/shard_map/prepare/pallas_call | solution.py:586
  25.1 0.0 collective-permute-done.refs_1_
  25.2 0.0 collective-permute-done.1.refs_2_
  25.2 0.0 collective-permute-done.2.refs_3_
  25.2 22.8 %pull.1 = f32[3,8192]{1,0:T(4,128)} custom-call(f32[8,16,128]{2,1,0:T(8,128)S(1)} %slice.4.refs_0_, f32[8,16,128]{2,1,0:T(8,128)S(1)} %collective-permute-done.refs_1_, f32[8,16,128]{2,1,0:T(8,128)S(1)} %collective-permute-done.1.refs_2_, f32[8,16,128]{2,1,0:T(8,128)S(1)} %collective-permute-done.2.refs_3_, f32[576,4,128]{2,1,0:T(4,128)S(1)} %get-tuple-element.19.refs_4_, ...), custom_call_target="tpu_custom_call" | custom-call | tf_op jit(solution)/shard_map/pull/pallas_call | solution.py:608
  (1 shorter events, 0.0 us)
Async XLA Ops:
  2.4 14.6 %all-to-all-start = ((f32[8,32,128]{2,1,0:T(8,128)}), f32[8,32,128]{2,1,0:T(8,128)S(1)}, u32[]{:S(2)}, u32[]{:S(2)}) async-start(f32[8,32,128]{2,1,0:T(8,128)} %get-tuple-element.16), calls=%async_computation | async-start | bytes 262144 | tf_op jit(solution)/shard_map/all_to_all | solution.py:575
  9.7 8.9 %collective-permute-start.3 = (f32[256,128]{1,0:T(8,128)}, f32[256,128]{1,0:T(8,128)S(1)}, u32[]{:S(2)}, u32[]{:S(2)}) collective-permute-start(f32[256,128]{1,0:T(8,128)} %get-tuple-element.18), channel_id=1, source_target_pairs={{0,1},{1,2},{2,3},{3,0},{4,5},{5,6},{6,7},{7,4},{8,9},{9,10},{10,1... | collective-permute-start | bytes 393224 | tf_op jit(solution)/shard_map/ppermute | solution.py:580
  9.7 10.3 %collective-permute-start.4 = (f32[256,128]{1,0:T(8,128)}, f32[256,128]{1,0:T(8,128)S(1)}, u32[]{:S(2)}, u32[]{:S(2)}) collective-permute-start(f32[256,128]{1,0:T(8,128)} %get-tuple-element.18), channel_id=1, source_target_pairs={{0,2},{1,3},{2,0},{3,1},{4,6},{5,7},{6,4},{7,5},{8,10},{9,11},{10,... | collective-permute-start | bytes 393224 | tf_op jit(solution)/shard_map/ppermute | solution.py:580
  11.3 8.8 %collective-permute-start.5 = (f32[256,128]{1,0:T(8,128)}, f32[256,128]{1,0:T(8,128)S(1)}, u32[]{:S(2)}, u32[]{:S(2)}) collective-permute-start(f32[256,128]{1,0:T(8,128)} %get-tuple-element.18), channel_id=1, source_target_pairs={{0,3},{1,0},{2,1},{3,2},{4,7},{5,4},{6,5},{7,6},{8,11},{9,8},{10,9... | collective-permute-start | bytes 393224 | tf_op jit(solution)/shard_map/ppermute | solution.py:580
  17.0 8.1 %collective-permute-start = (f32[8,16,128]{2,1,0:T(8,128)S(1)}, f32[8,16,128]{2,1,0:T(8,128)S(1)}, u32[]{:S(2)}, u32[]{:S(2)}) collective-permute-start(f32[8,16,128]{2,1,0:T(8,128)S(1)} %slice.4.refs_0_), channel_id=1, source_target_pairs={{0,1},{1,2},{2,3},{3,0},{4,5},{5,6},{6,7},{7,4},{8,9},{9,10},{10,1... | collective-permute-start | bytes 196616 | tf_op jit(solution)/shard_map/ppermute | solution.py:580
  17.0 8.1 %collective-permute-start.1 = (f32[8,16,128]{2,1,0:T(8,128)S(1)}, f32[8,16,128]{2,1,0:T(8,128)S(1)}, u32[]{:S(2)}, u32[]{:S(2)}) collective-permute-start(f32[8,16,128]{2,1,0:T(8,128)S(1)} %slice.4.refs_0_), channel_id=1, source_target_pairs={{0,2},{1,3},{2,0},{3,1},{4,6},{5,7},{6,4},{7,5},{8,10},{9,11},{10,... | collective-permute-start | bytes 196616 | tf_op jit(solution)/shard_map/ppermute | solution.py:580
  18.6 6.5 %collective-permute-start.2 = (f32[8,16,128]{2,1,0:T(8,128)S(1)}, f32[8,16,128]{2,1,0:T(8,128)S(1)}, u32[]{:S(2)}, u32[]{:S(2)}) collective-permute-start(f32[8,16,128]{2,1,0:T(8,128)S(1)} %slice.4.refs_0_), channel_id=1, source_target_pairs={{0,3},{1,0},{2,1},{3,2},{4,7},{5,4},{6,5},{7,6},{8,11},{9,8},{10,9... | collective-permute-start | bytes 196616 | tf_op jit(solution)/shard_map/ppermute | solution.py:580
  20.0 0.9 %copy-start = (f32[400,128]{1,0:T(8,128)S(1)}, f32[400,128]{1,0:T(8,128)}, u32[]{:S(2)}) copy-start(f32[400,128]{1,0:T(8,128)} %get-tuple-element.17.refs_0_) | copy-start | bytes 614404
where the time goes:
time: 48.3 us; the launch traced here: 48 us
  Pallas kernels  29.4 us (61%)
  starting transfers between devices  13.2 us (27%)
  waiting for transfers between devices  4.37 us (9%)
  local copies, waits for them, and re-layouts  0.93 us (2%)
    pallas_call x1, Pallas kernels, on_device(): pl.pallas_call(functools.partial(pull_kernel, n_dom, n_sub), out_shape=ja...  22.8 us
    all_to_all x1, starting transfers between devices, on_device(): lax.all_to_all(sent, 'dom', split_axis=0, concat_axis=0, tiled=True)  7.26 us
    ppermute x6, starting transfers between devices, around(): lax.ppermute(value, 'sub', [(seg, (seg + shift) % n_sub) for seg in range...  5.96 us
    all_to_all x1, waiting for transfers between devices, on_device(): lax.all_to_all(sent, 'dom', split_axis=0, concat_axis=0, tiled=True)  4.36 us
    pallas_call x1, Pallas kernels, on_device(): pl.pallas_call(functools.partial(prepare_kernel, n_dom, n_sub), out_shape...  4.18 us
    pallas_call x1, Pallas kernels, on_device(): pl.pallas_call(functools.partial(pack_kernel, n_dom), out_shape=(jax.Shap...  2.4 us
  transfers between devices with their start and end apart: 7, of which 1 were waited for; matrix products, arithmetic and copies ran while one was open for 0% of the time, Pallas kernels for 9%

commit v1 on v0

--- a/solution.py
+++ b/solution.py
@@ -29,13 +29,14 @@
 
 H_ROWS = 32
 Q_ROWS = 64
-V_ROWS = 16
-U_ROWS = 48
+V_ROWS = 8
+U_ROWS = 32
 Q_AT = H_ROWS
 V_AT = Q_AT + Q_ROWS
 U_AT = V_AT + V_ROWS
 CELL_ROWS = U_AT + U_ROWS
 M_ROWS = 8
+MOMENTS = V_ROWS + U_ROWS
 
 
 def rounded(value):
@@ -47,6 +48,11 @@
     rest = value - first
     second = rounded(rest)
     return first, second, rest - second
+
+
+def high_low(value):
+    high = rounded(value)
+    return high, value - high
 
 
 def two_parts(value):
@@ -93,8 +99,10 @@
     for copy in copies:
         copy.wait()
     put_own(pos_ref, mass_ref, out_ref)
+    results[0].start()
     out_ref[OWN_ROWS : OWN_ROWS + LEAF_DEV, :] = cl_ref[...].astype(F32)
     out_ref[OWN_ROWS + LEAF_DEV :, :] = ll_ref[...].astype(F32)
+    results[2].start()
 
     def put_cells(target, carry):
         sent_ref[target, OUT_ROWS : OUT_ROWS + 1, :] = cmass_ref[...]
@@ -115,8 +123,7 @@
         target = jnp.where((target >= 0) & (target < n_dom), target, n_dom)
         for unit in range(OUT_UNITS):
             sent_ref[target, 4 * unit : 4 * unit + 4, :] = jnp.where(left, half(slot, 2 * unit, 0), half(slot, 2 * unit + 1, 1))
-    for copy in results:
-        copy.start()
+    results[1].start()
     for copy in results:
         copy.wait()
 
@@ -189,7 +196,7 @@
     me = lax.axis_index("sub")
 
     def look_up(dom, shift, found):
-        here = owner == dom * n_sub + lax.rem(me + n_sub - shift, n_sub)
+        here = owner == dom * n_sub + lax.bitwise_xor(me, shift)
         new = []
         for comp in range(CELL_COMPS):
             value = jnp.take_along_axis(spread_ref[dom, shift, comp], lane, axis=1, mode="promise_in_bounds")
@@ -231,12 +238,12 @@
     put_rows(cf_ref, dict(enumerate(rows, Q_AT)))
     yield
     for comp, value in enumerate((cx, cy, cz)):
-        for which, part in enumerate(three_parts(value)):
+        for which, part in enumerate(high_low(value)):
             cf_ref[8 * (V_AT + 4 * which + comp) : 8 * (V_AT + 4 * which + comp) + 8, :] = part
     yield
-    columns = {name: three_parts(value) for name, value in dict(xx=xx, yy=yy, zz=zz, xy=xy, xz=xz, yz=yz, cx=qx, cy=qy, cz=qz).items()}
+    columns = {name: high_low(value) for name, value in dict(xx=xx, yy=yy, zz=zz, xy=xy, xz=xz, yz=yz, cx=qx, cy=qy, cz=qz).items()}
     order = (("xx", "xy", "xz"), ("xy", "yy", "yz"), ("xz", "yz", "zz"), ("cx", "cy", "cz"))
-    for which in range(3):
+    for which in range(2):
         for column, names in enumerate(order):
             for row, name in enumerate(names):
                 at = U_AT + 16 * which + 4 * column + row
@@ -253,8 +260,7 @@
     mass = value[3]
     centred = [value[comp] - ce_ref[comp, pl.ds(group, 1), :] for comp in range(3)]
     for comp, v in enumerate([mass * v for v in centred] + [mass]):
-        high = rounded(v)
-        for which, part in enumerate((high, v - high)):
+        for which, part in enumerate(high_low(v)):
             at = 4 * which + comp
             sf_ref[8 * at : 8 * at + 8, :] = part
 
@@ -284,13 +290,9 @@
     inv_two = inv * inv
     inv_three = inv * inv_two
     pull = inv_three * (cm_ref[pl.ds(sub, 1), :] + quad_form * (inv_two * inv_two))
-    moments = jnp.concatenate(
-        [
-            jnp.concatenate([cell_rows(V_AT, V_ROWS), jnp.zeros((V_ROWS, 128), BF16)], axis=1),
-            jnp.concatenate([jnp.zeros((U_ROWS, 128), BF16), cell_rows(U_AT, U_ROWS)], axis=1),
-        ],
-        axis=0,
-    )
+    moments = cf_ref[pl.ds(8 * V_AT + sub, MOMENTS, stride=8), :]
+    kind = lax.broadcasted_iota(jnp.int32, (MOMENTS, 128), 0) < V_ROWS
+    moments = jnp.concatenate([jnp.where(kind, moments, 0.0), jnp.where(kind, 0.0, moments)], axis=1)
     both = jnp.concatenate([stacked(pull), stacked(inv_three * inv_two)], axis=1)
     return both, moments
 
@@ -310,23 +312,34 @@
 
 def cell_pull(octet, tg_ref, ah_ref, cf_ref, cm_ref, out_ref):
     upper = lax.broadcasted_iota(jnp.int32, (8, 128), 0) < 4
-    left = lax.broadcasted_iota(jnp.int32, (LEAF, 128), 1) < LEAF
-    for inner in range(4):
-        pair = octet * 4 + inner
-        first, first_moments = cell_group(2 * inner, ah_ref[pair, 0:LEAF, :], cf_ref, cm_ref)
+    first_lanes = lax.broadcasted_iota(jnp.int32, (LEAF, 128), 1) < MOMENTS
+    padding = jnp.zeros((128 - 2 * MOMENTS, 256), F32)
+    for half in range(2):
+        both, moments = [], []
+        for group in range(4):
+            sub = 4 * half + group
+            rows = pl.ds(LEAF * (group % 2), LEAF)
+            weights, own_moments = cell_group(sub, ah_ref[octet * 4 + sub // 2, rows, :], cf_ref, cm_ref)
+            both.append(weights)
+            moments.append(own_moments)
+            if group % 2 == 1:
+                moments.append(padding)
+            yield
+        moments = jnp.concatenate(moments, axis=0).astype(BF16)
+        totals = transposed_dot(jnp.concatenate(both, axis=0), moments)
         yield
-        second, second_moments = cell_group(2 * inner + 1, ah_ref[pair, LEAF:, :], cf_ref, cm_ref)
-        moments = jnp.concatenate([first_moments, second_moments], axis=0)
-        sums = transposed_dot(jnp.concatenate([first, second], axis=0), moments)
-        yield
-        sums = jnp.where(left, sums[0:64] + sums[64:128], sums[128:192] + sums[192:256]).T
-        sums = jnp.concatenate([sums[0:64], sums[64:128]], axis=1)
-        place = pair_place(tg_ref, pair)
-        x, y, z = [place[comp : comp + 1, :] for comp in range(3)]
-        quads = sums[16:32] + sums[32:48] + sums[48:64]
-        turned = quads[0:8] * jnp.where(upper, x, y) + quads[8:16] * jnp.where(upper, z, -1.0)
-        turned = turned + pltpu.roll(turned, 4, 0)
-        out_ref[:, pair_lanes(pair)] = point_sums(sums[0:8] + sums[8:16], place) + turned[0:3]
+        for side in range(2):
+            pair = octet * 4 + 2 * half + side
+            at, columns = 256 * side, slice(128 * side, 128 * side + 128)
+            sums = [totals[row : row + LEAF, columns] + totals[row + LEAF : row + 128, columns] for row in (at, at + 128)]
+            sums = jnp.where(first_lanes, sums[0], sums[1]).T
+            sums = jnp.concatenate([sums[0:MOMENTS], sums[MOMENTS : 2 * MOMENTS]], axis=1)
+            place = pair_place(tg_ref, pair)
+            x, y, z = [place[comp : comp + 1, :] for comp in range(3)]
+            quads = sums[V_ROWS : V_ROWS + 16] + sums[V_ROWS + 16 :]
+            turned = quads[0:8] * jnp.where(upper, x, y) + quads[8:16] * jnp.where(upper, z, -1.0)
+            turned = turned + pltpu.roll(turned, 4, 0)
+            out_ref[:, pair_lanes(pair)] = point_sums(sums[0:V_ROWS], place) + turned[0:3]
 
 
 def put_block_pair(tab_ref, block, value):
@@ -356,7 +369,7 @@
     me = lax.axis_index("sub")
 
     def near_blocks(shift, near_ref):
-        seg = lax.rem(me + n_sub - shift, n_sub)
+        seg = lax.bitwise_xor(me, shift)
 
         def near(step, carry):
             for at in range(8):
@@ -441,8 +454,6 @@
 
     lax.fori_loop(0, n_dom, spread, 0)
 
-    run(build(0))
-    copy.wait()
     left = lax.broadcasted_iota(jnp.int32, (M_ROWS, 128), 1) < LEAF
     left_target = lax.broadcasted_iota(jnp.int32, (H_ROWS, 128), 1) < LEAF
     owner = (lax.broadcasted_iota(jnp.int32, (LEAF, 128), 1) // H_ROWS).astype(BF16)
@@ -494,8 +505,16 @@
             out_ref[:, lanes] = out_ref[:, lanes] + point_sums(sums, pair_place(tg_ref, pair))
 
     quads, octets = LEAF_DEV // 4, LEAF_DEV // 8
-    run(features(0, 0, even_ref))
-    run(distances(0, dist_even))
+    copy.wait()
+    first, moments, distance = build(0), features(0, 0, even_ref), distances(0, dist_even)
+    for step in range(4):
+        run(first, 8)
+        run(moments, 1)
+        if step % 2 == 0:
+            run(distance, 1)
+    run(first)
+    run(moments)
+    run(distance)
 
     def one_octet(octet, carry):
         quad = 2 * octet
@@ -574,14 +593,17 @@
     )(*ins)
     received = lax.all_to_all(sent, "dom", split_axis=0, concat_axis=0, tiled=True)
 
-    def around(value):
-        pieces = [value]
-        for shift in range(1, n_sub):
-            pieces.append(lax.ppermute(value, "sub", [(seg, (seg + shift) % n_sub) for seg in range(n_sub)]))
-        return pieces
-
-    nearby = around(packed)
-    cells = around(received[:, OUT_ROWS:])
+    def across(value, bits):
+        return lax.ppermute(value, "sub", [(seg, seg ^ bits) for seg in range(n_sub)])
+
+    nearby = {0: packed}
+    bit = n_sub // 2
+    while bit:
+        nearby.update({at ^ bit: across(value, bit) for at, value in nearby.items()})
+        bit //= 2
+    nearby = [nearby[at] for at in range(n_sub)]
+    own_cells = received[:, OUT_ROWS:]
+    cells = [own_cells] + [across(own_cells, bits) for bits in range(1, n_sub)]
     n_blocks = n_sub * LEAF_DEV + 2 * RANGE * CAP
     prepared = pl.pallas_call(
         functools.partial(prepare_kernel, n_dom, n_sub),

time: 48.3 us -> 49.9 us (1.033)
  Pallas kernels: 29.4 us -> 32.2 us
  starting transfers between devices: 13.2 us -> 10.6 us
  waiting for transfers between devices: 4.37 us -> 5.83 us
    ppermute x6, waiting for transfers between devices: 0.02 us -> 3.67 us  [across(): lax.ppermute(value, 'sub', [(seg, seg ^ bits) for seg in range(n_sub)])]
    pallas_call x1, Pallas kernels: 22.8 us -> 25.4 us  [on_device(): pl.pallas_call(functools.partial(pull_kernel, n_dom, n_sub), out_shape=ja...]
    ppermute x6, starting transfers between devices: 5.96 us -> 3.38 us  [across(): lax.ppermute(value, 'sub', [(seg, seg ^ bits) for seg in range(n_sub)])]
    all_to_all x1, waiting for transfers between devices: 4.36 us -> 2.16 us  [on_device(): lax.all_to_all(sent, 'dom', split_axis=0, concat_axis=0, tiled=True)]
  transfers between devices with their start and end apart: 7 -> 7, of which waited for: 1 -> 2; matrix products, arithmetic and copies ran while one was open for 0% -> 0% of each run, Pallas kernels for 9% -> 9%
where the time goes in v1:
time: 49.9 us; the launch traced here: 49.6 us
  Pallas kernels  32.2 us (65%)
  starting transfers between devices  10.6 us (21%)
  waiting for transfers between devices  5.83 us (12%)
  local copies, waits for them, and re-layouts  0.93 us (2%)
    pallas_call x1, Pallas kernels, on_device(): pl.pallas_call(functools.partial(pull_kernel, n_dom, n_sub), out_shape=ja...  25.4 us
    all_to_all x1, starting transfers between devices, on_device(): lax.all_to_all(sent, 'dom', split_axis=0, concat_axis=0, tiled=True)  7.26 us
    pallas_call x1, Pallas kernels, on_device(): pl.pallas_call(functools.partial(prepare_kernel, n_dom, n_sub), out_shape...  4.46 us
    ppermute x6, waiting for transfers between devices, across(): lax.ppermute(value, 'sub', [(seg, seg ^ bits) for seg in range(n_sub)])  3.67 us
    ppermute x6, starting transfers between devices, across(): lax.ppermute(value, 'sub', [(seg, seg ^ bits) for seg in range(n_sub)])  3.38 us
    pallas_call x1, Pallas kernels, on_device(): pl.pallas_call(functools.partial(pack_kernel, n_dom), out_shape=(jax.Shap...  2.29 us
    all_to_all x1, waiting for transfers between devices, on_device(): lax.all_to_all(sent, 'dom', split_axis=0, concat_axis=0, tiled=True)  2.16 us
  transfers between devices with their start and end apart: 7, of which 2 were waited for; matrix products, arithmetic and copies ran while one was open for 0% of the time, Pallas kernels for 9%

profile of v1, /device:TPU:0, one launch (start us, length us, event | category | flops | bytes accessed | tf_op | source)
XLA Modules:
  0.0 49.6 jit_solution(4190288712419998061)
XLA Ops:
  0.0 2.3 %pack_own.1 = (f32[256,128]{1,0:T(8,128)}, f32[8,32,128]{2,1,0:T(8,128)}, f32[400,128]{1,0:T(8,128)}) custom-call(f32[3,8192]{1,0:T(4,128)} %refs_0_.1, f32[1,8192]{1,0:T(1,128)} %bitcast.5, f32[1,128]{1,0:T(1,128)} %bitcast.8, f32[3,128]{1,0:T(4,128)} %refs_3_.1, f32[6,128]{1,0:T(8,128)} %refs_4_.1, s32[128,128]{1,0:T(8,128)} %refs_5_.1, ...), custom_call_target="tpu_custom_call" | custom-call | tf_op jit(solution)/shard_map/pack_own/pallas_call | solution.py:575
  2.3 7.3 %all-to-all-start = ((f32[8,32,128]{2,1,0:T(8,128)}), f32[8,32,128]{2,1,0:T(8,128)S(1)}, u32[]{:S(2)}, u32[]{:S(2)}) async-start(f32[8,32,128]{2,1,0:T(8,128)} %get-tuple-element.16), calls=%async_computation | async-start | bytes 262144 | tf_op jit(solution)/shard_map/all_to_all | solution.py:594
  9.6 1.5 %collective-permute-start.4 = (f32[256,128]{1,0:T(8,128)}, f32[256,128]{1,0:T(8,128)S(1)}, u32[]{:S(2)}, u32[]{:S(2)}) collective-permute-start(f32[256,128]{1,0:T(8,128)} %get-tuple-element.18), channel_id=1, source_target_pairs={{0,2},{1,3},{2,0},{3,1},{4,6},{5,7},{6,4},{7,5},{8,10},{9,11},{10,... | collective-permute-start | bytes 393224 | tf_op jit(solution)/shard_map/ppermute | solution.py:597
  11.1 0.0 collective-permute-start.3
  11.1 3.7 %collective-permute-done.4.refs_2_ = f32[256,128]{1,0:T(8,128)S(1)} collective-permute-done((f32[256,128]{1,0:T(8,128)}, f32[256,128]{1,0:T(8,128)S(1)}, u32[]{:S(2)}, u32[]{:S(2)}) %collective-permute-start.4) | collective-permute-done | bytes 131104 | tf_op jit(solution)/shard_map/ppermute | solution.py:597
  14.7 0.0 collective-permute-start.5
  14.7 2.2 %all-to-all-done.refs_4_ = f32[8,32,128]{2,1,0:T(8,128)S(1)} async-done(((f32[8,32,128]{2,1,0:T(8,128)}), f32[8,32,128]{2,1,0:T(8,128)S(1)}, u32[]{:S(2)}, u32[]{:S(2)}) %all-to-all-start) | async-done | bytes 131104 | tf_op jit(solution)/shard_map/all_to_all | solution.py:594
  16.9 0.0 collective-permute-start
  16.9 1.6 %collective-permute-start.1 = (f32[8,16,128]{2,1,0:T(8,128)S(1)}, f32[8,16,128]{2,1,0:T(8,128)S(1)}, u32[]{:S(2)}, u32[]{:S(2)}) collective-permute-start(f32[8,16,128]{2,1,0:T(8,128)S(1)} %slice.4.refs_0_), channel_id=1, source_target_pairs={{0,2},{1,3},{2,0},{3,1},{4,6},{5,7},{6,4},{7,5},{8,10},{9,11},{10,... | collective-permute-start | bytes 196616 | tf_op jit(solution)/shard_map/ppermute | solution.py:597
  18.5 0.3 collective-permute-start.2
  18.8 0.0 collective-permute-done.3.refs_1_
  18.8 0.0 collective-permute-done.5.refs_3_
  18.8 0.0 copy-start
  18.8 0.9 %copy-done = f32[400,128]{1,0:T(8,128)S(1)} copy-done((f32[400,128]{1,0:T(8,128)S(1)}, f32[400,128]{1,0:T(8,128)}, u32[]{:S(2)}) %copy-start) | copy-done | bytes 204824
  19.7 4.5 %prepare.1 = (f32[576,4,128]{2,1,0:T(4,128)S(1)}, bf16[576,64,128]{2,1,0:T(8,128)(2,1)S(1)}, bf16[64,32,128]{2,1,0:T(8,128)(2,1)S(1)}, f32[256,128]{1,0:T(8,128)...) custom-call(f32[400,128]{1,0:T(8,128)S(1)} %copy-done, ...), custom_call_target="tpu_custom_call" | custom-call | bytes 20000000 | tf_op jit(solution)/shard_map/prepare/pallas_call | solution.py:608
  24.2 0.0 collective-permute-done.refs_1_
  24.2 0.0 collective-permute-done.1.refs_2_
  24.2 0.0 collective-permute-done.2.refs_3_
  24.2 25.4 %pull.1 = f32[3,8192]{1,0:T(4,128)} custom-call(f32[8,16,128]{2,1,0:T(8,128)S(1)} %slice.4.refs_0_, f32[8,16,128]{2,1,0:T(8,128)S(1)} %collective-permute-done.refs_1_, f32[8,16,128]{2,1,0:T(8,128)S(1)} %collective-permute-done.1.refs_2_, f32[8,16,128]{2,1,0:T(8,128)S(1)} %collective-permute-done.2.refs_3_, f32[576,4,128]{2,1,0:T(4,128)S(1)} %get-tuple-element.19.refs_4_, ...), custom_call_target="tpu_custom_call" | custom-call | tf_op jit(solution)/shard_map/pull/pallas_call | solution.py:630
  (1 shorter events, 0.0 us)
Async XLA Ops:
  2.3 14.6 %all-to-all-start = ((f32[8,32,128]{2,1,0:T(8,128)}), f32[8,32,128]{2,1,0:T(8,128)S(1)}, u32[]{:S(2)}, u32[]{:S(2)}) async-start(f32[8,32,128]{2,1,0:T(8,128)} %get-tuple-element.16), calls=%async_computation | async-start | bytes 262144 | tf_op jit(solution)/shard_map/all_to_all | solution.py:594
  9.6 5.2 %collective-permute-start.4 = (f32[256,128]{1,0:T(8,128)}, f32[256,128]{1,0:T(8,128)S(1)}, u32[]{:S(2)}, u32[]{:S(2)}) collective-permute-start(f32[256,128]{1,0:T(8,128)} %get-tuple-element.18), channel_id=1, source_target_pairs={{0,2},{1,3},{2,0},{3,1},{4,6},{5,7},{6,4},{7,5},{8,10},{9,11},{10,... | collective-permute-start | bytes 393224 | tf_op jit(solution)/shard_map/ppermute | solution.py:597
  11.1 7.7 %collective-permute-start.3 = (f32[256,128]{1,0:T(8,128)}, f32[256,128]{1,0:T(8,128)S(1)}, u32[]{:S(2)}, u32[]{:S(2)}) collective-permute-start(f32[256,128]{1,0:T(8,128)} %get-tuple-element.18), channel_id=1, source_target_pairs={{0,1},{1,0},{2,3},{3,2},{4,5},{5,4},{6,7},{7,6},{8,9},{9,8},{10,11... | collective-permute-start | bytes 393224 | tf_op jit(solution)/shard_map/ppermute | solution.py:597
  14.7 4.0 %collective-permute-start.5 = (f32[256,128]{1,0:T(8,128)S(1)}, f32[256,128]{1,0:T(8,128)S(1)}, u32[]{:S(2)}, u32[]{:S(2)}) collective-permute-start(f32[256,128]{1,0:T(8,128)S(1)} %collective-permute-done.4.refs_2_), channel_id=1, source_target_pairs={{0,1},{1,0},{2,3},{3,2},{4,5},{5,4},{6,7},{7,6},{8,9},{9,8},{10,11... | collective-permute-start | bytes 393224 | tf_op jit(solution)/shard_map/ppermute | solution.py:597
  16.9 7.3 %collective-permute-start = (f32[8,16,128]{2,1,0:T(8,128)S(1)}, f32[8,16,128]{2,1,0:T(8,128)S(1)}, u32[]{:S(2)}, u32[]{:S(2)}) collective-permute-start(f32[8,16,128]{2,1,0:T(8,128)S(1)} %slice.4.refs_0_), channel_id=1, source_target_pairs={{0,1},{1,0},{2,3},{3,2},{4,5},{5,4},{6,7},{7,6},{8,9},{9,8},{10,11... | collective-permute-start | bytes 196616 | tf_op jit(solution)/shard_map/ppermute | solution.py:597
  16.9 7.3 %collective-permute-start.1 = (f32[8,16,128]{2,1,0:T(8,128)S(1)}, f32[8,16,128]{2,1,0:T(8,128)S(1)}, u32[]{:S(2)}, u32[]{:S(2)}) collective-permute-start(f32[8,16,128]{2,1,0:T(8,128)S(1)} %slice.4.refs_0_), channel_id=1, source_target_pairs={{0,2},{1,3},{2,0},{3,1},{4,6},{5,7},{6,4},{7,5},{8,10},{9,11},{10,... | collective-permute-start | bytes 196616 | tf_op jit(solution)/shard_map/ppermute | solution.py:597
  18.5 5.7 %collective-permute-start.2 = (f32[8,16,128]{2,1,0:T(8,128)S(1)}, f32[8,16,128]{2,1,0:T(8,128)S(1)}, u32[]{:S(2)}, u32[]{:S(2)}) collective-permute-start(f32[8,16,128]{2,1,0:T(8,128)S(1)} %slice.4.refs_0_), channel_id=1, source_target_pairs={{0,3},{1,2},{2,1},{3,0},{4,7},{5,6},{6,5},{7,4},{8,11},{9,10},{10,... | collective-permute-start | bytes 196616 | tf_op jit(solution)/shard_map/ppermute | solution.py:597
  18.8 0.9 %copy-start = (f32[400,128]{1,0:T(8,128)S(1)}, f32[400,128]{1,0:T(8,128)}, u32[]{:S(2)}) copy-start(f32[400,128]{1,0:T(8,128)} %get-tuple-element.17.refs_0_) | copy-start | bytes 614404

commit v2 on v0

--- a/solution.py
+++ b/solution.py
@@ -47,6 +47,11 @@
     rest = value - first
     second = rounded(rest)
     return first, second, rest - second
+
+
+def high_low(value):
+    high = rounded(value)
+    return high, value - high
 
 
 def two_parts(value):
@@ -93,8 +98,10 @@
     for copy in copies:
         copy.wait()
     put_own(pos_ref, mass_ref, out_ref)
+    results[0].start()
     out_ref[OWN_ROWS : OWN_ROWS + LEAF_DEV, :] = cl_ref[...].astype(F32)
     out_ref[OWN_ROWS + LEAF_DEV :, :] = ll_ref[...].astype(F32)
+    results[2].start()
 
     def put_cells(target, carry):
         sent_ref[target, OUT_ROWS : OUT_ROWS + 1, :] = cmass_ref[...]
@@ -115,8 +122,7 @@
         target = jnp.where((target >= 0) & (target < n_dom), target, n_dom)
         for unit in range(OUT_UNITS):
             sent_ref[target, 4 * unit : 4 * unit + 4, :] = jnp.where(left, half(slot, 2 * unit, 0), half(slot, 2 * unit + 1, 1))
-    for copy in results:
-        copy.start()
+    results[1].start()
     for copy in results:
         copy.wait()
 
@@ -189,7 +195,7 @@
     me = lax.axis_index("sub")
 
     def look_up(dom, shift, found):
-        here = owner == dom * n_sub + lax.rem(me + n_sub - shift, n_sub)
+        here = owner == dom * n_sub + lax.bitwise_xor(me, shift)
         new = []
         for comp in range(CELL_COMPS):
             value = jnp.take_along_axis(spread_ref[dom, shift, comp], lane, axis=1, mode="promise_in_bounds")
@@ -253,8 +259,7 @@
     mass = value[3]
     centred = [value[comp] - ce_ref[comp, pl.ds(group, 1), :] for comp in range(3)]
     for comp, v in enumerate([mass * v for v in centred] + [mass]):
-        high = rounded(v)
-        for which, part in enumerate((high, v - high)):
+        for which, part in enumerate(high_low(v)):
             at = 4 * which + comp
             sf_ref[8 * at : 8 * at + 8, :] = part
 
@@ -356,7 +361,7 @@
     me = lax.axis_index("sub")
 
     def near_blocks(shift, near_ref):
-        seg = lax.rem(me + n_sub - shift, n_sub)
+        seg = lax.bitwise_xor(me, shift)
 
         def near(step, carry):
             for at in range(8):
@@ -441,8 +446,6 @@
 
     lax.fori_loop(0, n_dom, spread, 0)
 
-    run(build(0))
-    copy.wait()
     left = lax.broadcasted_iota(jnp.int32, (M_ROWS, 128), 1) < LEAF
     left_target = lax.broadcasted_iota(jnp.int32, (H_ROWS, 128), 1) < LEAF
     owner = (lax.broadcasted_iota(jnp.int32, (LEAF, 128), 1) // H_ROWS).astype(BF16)
@@ -471,11 +474,8 @@
             low = jnp.where(first_own, rows[0], rows[1])
             high = jnp.where(third_own, rows[2], rows[3])
             sources.append(jnp.where(lower_half, low, high))
-            if j % 8 == 7:
-                rows = pl.ds(LEAF * (j - 7), 8 * LEAF)
-                dist_ref[rows, :] = jnp.dot(jnp.concatenate(sources, axis=0), targets, preferred_element_type=F32)
-                sources = []
-                yield
+        dist_ref[...] = jnp.dot(jnp.concatenate(sources, axis=0), targets, preferred_element_type=F32)
+        yield
 
     def pull(quad, slot_ref, dist_ref):
         total = jnp.zeros((4 * M_ROWS, 256), F32)
@@ -494,8 +494,16 @@
             out_ref[:, lanes] = out_ref[:, lanes] + point_sums(sums, pair_place(tg_ref, pair))
 
     quads, octets = LEAF_DEV // 4, LEAF_DEV // 8
-    run(features(0, 0, even_ref))
-    run(distances(0, dist_even))
+    copy.wait()
+    first, moments, distance = build(0), features(0, 0, even_ref), distances(0, dist_even)
+    for step in range(4):
+        run(first, 8)
+        run(moments, 1)
+        if step % 2 == 0:
+            run(distance, 1)
+    run(first)
+    run(moments)
+    run(distance)
 
     def one_octet(octet, carry):
         quad = 2 * octet
@@ -511,7 +519,7 @@
             direct = pull(now, slot_ref, dist_ref)
             moments, distance = features(ahead, raw_at, ahead_slot), distances(ahead, ahead_dist)
             for step in range(8):
-                if step in (1, 4):
+                if step == 1:
                     run(distance, 1)
                 run(direct, 1)
                 if step % 2 == 0:
@@ -574,14 +582,17 @@
     )(*ins)
     received = lax.all_to_all(sent, "dom", split_axis=0, concat_axis=0, tiled=True)
 
-    def around(value):
-        pieces = [value]
-        for shift in range(1, n_sub):
-            pieces.append(lax.ppermute(value, "sub", [(seg, (seg + shift) % n_sub) for seg in range(n_sub)]))
-        return pieces
-
-    nearby = around(packed)
-    cells = around(received[:, OUT_ROWS:])
+    def across(value, bits):
+        return lax.ppermute(value, "sub", [(seg, seg ^ bits) for seg in range(n_sub)])
+
+    nearby = {0: packed}
+    bit = n_sub // 2
+    while bit:
+        nearby.update({at ^ bit: across(value, bit) for at, value in nearby.items()})
+        bit //= 2
+    nearby = [nearby[at] for at in range(n_sub)]
+    own_cells = received[:, OUT_ROWS:]
+    cells = [own_cells] + [across(own_cells, bits) for bits in range(1, n_sub)]
     n_blocks = n_sub * LEAF_DEV + 2 * RANGE * CAP
     prepared = pl.pallas_call(
         functools.partial(prepare_kernel, n_dom, n_sub),

time: 48.3 us -> 49 us (1.014)
  starting transfers between devices: 13.2 us -> 10.6 us
  Pallas kernels: 29.4 us -> 31.3 us
  waiting for transfers between devices: 4.37 us -> 5.83 us
    ppermute x6, waiting for transfers between devices: 0.02 us -> 3.67 us  [across(): lax.ppermute(value, 'sub', [(seg, seg ^ bits) for seg in range(n_sub)])]
    ppermute x6, starting transfers between devices: 5.96 us -> 3.38 us  [across(): lax.ppermute(value, 'sub', [(seg, seg ^ bits) for seg in range(n_sub)])]
    all_to_all x1, waiting for transfers between devices: 4.36 us -> 2.16 us  [on_device(): lax.all_to_all(sent, 'dom', split_axis=0, concat_axis=0, tiled=True)]
    pallas_call x1, Pallas kernels: 22.8 us -> 24.6 us  [on_device(): pl.pallas_call(functools.partial(pull_kernel, n_dom, n_sub), out_shape=ja...]
  transfers between devices with their start and end apart: 7 -> 7, of which waited for: 1 -> 2; matrix products, arithmetic and copies ran while one was open for 0% -> 0% of each run, Pallas kernels for 9% -> 9%
where the time goes in v2:
time: 49 us; the launch traced here: 48.8 us
  Pallas kernels  31.3 us (64%)
  starting transfers between devices  10.6 us (22%)
  waiting for transfers between devices  5.83 us (12%)
  local copies, waits for them, and re-layouts  0.93 us (2%)
    pallas_call x1, Pallas kernels, on_device(): pl.pallas_call(functools.partial(pull_kernel, n_dom, n_sub), out_shape=ja...  24.6 us
    all_to_all x1, starting transfers between devices, on_device(): lax.all_to_all(sent, 'dom', split_axis=0, concat_axis=0, tiled=True)  7.26 us
    pallas_call x1, Pallas kernels, on_device(): pl.pallas_call(functools.partial(prepare_kernel, n_dom, n_sub), out_shape...  4.46 us
    ppermute x6, waiting for transfers between devices, across(): lax.ppermute(value, 'sub', [(seg, seg ^ bits) for seg in range(n_sub)])  3.67 us
    ppermute x6, starting transfers between devices, across(): lax.ppermute(value, 'sub', [(seg, seg ^ bits) for seg in range(n_sub)])  3.38 us
    pallas_call x1, Pallas kernels, on_device(): pl.pallas_call(functools.partial(pack_kernel, n_dom), out_shape=(jax.Shap...  2.29 us
    all_to_all x1, waiting for transfers between devices, on_device(): lax.all_to_all(sent, 'dom', split_axis=0, concat_axis=0, tiled=True)  2.16 us
  transfers between devices with their start and end apart: 7, of which 2 were waited for; matrix products, arithmetic and copies ran while one was open for 0% of the time, Pallas kernels for 9%

profile of v2, /device:TPU:0, one launch (start us, length us, event | category | flops | bytes accessed | tf_op | source)
XLA Modules:
  0.0 48.8 jit_solution(17940627625660211793)
XLA Ops:
  0.0 2.3 %pack_own.1 = (f32[256,128]{1,0:T(8,128)}, f32[8,32,128]{2,1,0:T(8,128)}, f32[400,128]{1,0:T(8,128)}) custom-call(f32[3,8192]{1,0:T(4,128)} %refs_0_.1, f32[1,8192]{1,0:T(1,128)} %bitcast.5, f32[1,128]{1,0:T(1,128)} %bitcast.8, f32[3,128]{1,0:T(4,128)} %refs_3_.1, f32[6,128]{1,0:T(8,128)} %refs_4_.1, s32[128,128]{1,0:T(8,128)} %refs_5_.1, ...), custom_call_target="tpu_custom_call" | custom-call | tf_op jit(solution)/shard_map/pack_own/pallas_call | solution.py:564
  2.3 7.3 %all-to-all-start = ((f32[8,32,128]{2,1,0:T(8,128)}), f32[8,32,128]{2,1,0:T(8,128)S(1)}, u32[]{:S(2)}, u32[]{:S(2)}) async-start(f32[8,32,128]{2,1,0:T(8,128)} %get-tuple-element.16), calls=%async_computation | async-start | bytes 262144 | tf_op jit(solution)/shard_map/all_to_all | solution.py:583
  9.6 1.5 %collective-permute-start.4 = (f32[256,128]{1,0:T(8,128)}, f32[256,128]{1,0:T(8,128)S(1)}, u32[]{:S(2)}, u32[]{:S(2)}) collective-permute-start(f32[256,128]{1,0:T(8,128)} %get-tuple-element.18), channel_id=1, source_target_pairs={{0,2},{1,3},{2,0},{3,1},{4,6},{5,7},{6,4},{7,5},{8,10},{9,11},{10,... | collective-permute-start | bytes 393224 | tf_op jit(solution)/shard_map/ppermute | solution.py:586
  11.1 0.0 collective-permute-start.3
  11.1 3.7 %collective-permute-done.4.refs_2_ = f32[256,128]{1,0:T(8,128)S(1)} collective-permute-done((f32[256,128]{1,0:T(8,128)}, f32[256,128]{1,0:T(8,128)S(1)}, u32[]{:S(2)}, u32[]{:S(2)}) %collective-permute-start.4) | collective-permute-done | bytes 131104 | tf_op jit(solution)/shard_map/ppermute | solution.py:586
  14.7 0.0 collective-permute-start.5
  14.7 2.2 %all-to-all-done.refs_4_ = f32[8,32,128]{2,1,0:T(8,128)S(1)} async-done(((f32[8,32,128]{2,1,0:T(8,128)}), f32[8,32,128]{2,1,0:T(8,128)S(1)}, u32[]{:S(2)}, u32[]{:S(2)}) %all-to-all-start) | async-done | bytes 131104 | tf_op jit(solution)/shard_map/all_to_all | solution.py:583
  16.9 0.0 collective-permute-start
  16.9 1.6 %collective-permute-start.1 = (f32[8,16,128]{2,1,0:T(8,128)S(1)}, f32[8,16,128]{2,1,0:T(8,128)S(1)}, u32[]{:S(2)}, u32[]{:S(2)}) collective-permute-start(f32[8,16,128]{2,1,0:T(8,128)S(1)} %slice.4.refs_0_), channel_id=1, source_target_pairs={{0,2},{1,3},{2,0},{3,1},{4,6},{5,7},{6,4},{7,5},{8,10},{9,11},{10,... | collective-permute-start | bytes 196616 | tf_op jit(solution)/shard_map/ppermute | solution.py:586
  18.5 0.3 collective-permute-start.2
  18.8 0.0 collective-permute-done.3.refs_1_
  18.8 0.0 collective-permute-done.5.refs_3_
  18.8 0.0 copy-start
  18.8 0.9 %copy-done = f32[400,128]{1,0:T(8,128)S(1)} copy-done((f32[400,128]{1,0:T(8,128)S(1)}, f32[400,128]{1,0:T(8,128)}, u32[]{:S(2)}) %copy-start) | copy-done | bytes 204824
  19.7 4.5 %prepare.1 = (f32[576,4,128]{2,1,0:T(4,128)S(1)}, bf16[576,64,128]{2,1,0:T(8,128)(2,1)S(1)}, bf16[64,32,128]{2,1,0:T(8,128)(2,1)S(1)}, f32[256,128]{1,0:T(8,128)...) custom-call(f32[400,128]{1,0:T(8,128)S(1)} %copy-done, ...), custom_call_target="tpu_custom_call" | custom-call | bytes 20000000 | tf_op jit(solution)/shard_map/prepare/pallas_call | solution.py:597
  24.2 0.0 collective-permute-done.refs_1_
  24.2 0.0 collective-permute-done.1.refs_2_
  24.2 0.0 collective-permute-done.2.refs_3_
  24.2 24.6 %pull.1 = f32[3,8192]{1,0:T(4,128)} custom-call(f32[8,16,128]{2,1,0:T(8,128)S(1)} %slice.4.refs_0_, f32[8,16,128]{2,1,0:T(8,128)S(1)} %collective-permute-done.refs_1_, f32[8,16,128]{2,1,0:T(8,128)S(1)} %collective-permute-done.1.refs_2_, f32[8,16,128]{2,1,0:T(8,128)S(1)} %collective-permute-done.2.refs_3_, f32[576,4,128]{2,1,0:T(4,128)S(1)} %get-tuple-element.19.refs_4_, ...), custom_call_target="tpu_custom_call" | custom-call | tf_op jit(solution)/shard_map/pull/pallas_call | solution.py:619
  (1 shorter events, 0.0 us)
Async XLA Ops:
  2.3 14.6 %all-to-all-start = ((f32[8,32,128]{2,1,0:T(8,128)}), f32[8,32,128]{2,1,0:T(8,128)S(1)}, u32[]{:S(2)}, u32[]{:S(2)}) async-start(f32[8,32,128]{2,1,0:T(8,128)} %get-tuple-element.16), calls=%async_computation | async-start | bytes 262144 | tf_op jit(solution)/shard_map/all_to_all | solution.py:583
  9.6 5.2 %collective-permute-start.4 = (f32[256,128]{1,0:T(8,128)}, f32[256,128]{1,0:T(8,128)S(1)}, u32[]{:S(2)}, u32[]{:S(2)}) collective-permute-start(f32[256,128]{1,0:T(8,128)} %get-tuple-element.18), channel_id=1, source_target_pairs={{0,2},{1,3},{2,0},{3,1},{4,6},{5,7},{6,4},{7,5},{8,10},{9,11},{10,... | collective-permute-start | bytes 393224 | tf_op jit(solution)/shard_map/ppermute | solution.py:586
  11.1 7.7 %collective-permute-start.3 = (f32[256,128]{1,0:T(8,128)}, f32[256,128]{1,0:T(8,128)S(1)}, u32[]{:S(2)}, u32[]{:S(2)}) collective-permute-start(f32[256,128]{1,0:T(8,128)} %get-tuple-element.18), channel_id=1, source_target_pairs={{0,1},{1,0},{2,3},{3,2},{4,5},{5,4},{6,7},{7,6},{8,9},{9,8},{10,11... | collective-permute-start | bytes 393224 | tf_op jit(solution)/shard_map/ppermute | solution.py:586
  14.7 4.0 %collective-permute-start.5 = (f32[256,128]{1,0:T(8,128)S(1)}, f32[256,128]{1,0:T(8,128)S(1)}, u32[]{:S(2)}, u32[]{:S(2)}) collective-permute-start(f32[256,128]{1,0:T(8,128)S(1)} %collective-permute-done.4.refs_2_), channel_id=1, source_target_pairs={{0,1},{1,0},{2,3},{3,2},{4,5},{5,4},{6,7},{7,6},{8,9},{9,8},{10,11... | collective-permute-start | bytes 393224 | tf_op jit(solution)/shard_map/ppermute | solution.py:586
  16.9 7.3 %collective-permute-start = (f32[8,16,128]{2,1,0:T(8,128)S(1)}, f32[8,16,128]{2,1,0:T(8,128)S(1)}, u32[]{:S(2)}, u32[]{:S(2)}) collective-permute-start(f32[8,16,128]{2,1,0:T(8,128)S(1)} %slice.4.refs_0_), channel_id=1, source_target_pairs={{0,1},{1,0},{2,3},{3,2},{4,5},{5,4},{6,7},{7,6},{8,9},{9,8},{10,11... | collective-permute-start | bytes 196616 | tf_op jit(solution)/shard_map/ppermute | solution.py:586
  16.9 7.3 %collective-permute-start.1 = (f32[8,16,128]{2,1,0:T(8,128)S(1)}, f32[8,16,128]{2,1,0:T(8,128)S(1)}, u32[]{:S(2)}, u32[]{:S(2)}) collective-permute-start(f32[8,16,128]{2,1,0:T(8,128)S(1)} %slice.4.refs_0_), channel_id=1, source_target_pairs={{0,2},{1,3},{2,0},{3,1},{4,6},{5,7},{6,4},{7,5},{8,10},{9,11},{10,... | collective-permute-start | bytes 196616 | tf_op jit(solution)/shard_map/ppermute | solution.py:586
  18.5 5.7 %collective-permute-start.2 = (f32[8,16,128]{2,1,0:T(8,128)S(1)}, f32[8,16,128]{2,1,0:T(8,128)S(1)}, u32[]{:S(2)}, u32[]{:S(2)}) collective-permute-start(f32[8,16,128]{2,1,0:T(8,128)S(1)} %slice.4.refs_0_), channel_id=1, source_target_pairs={{0,3},{1,2},{2,1},{3,0},{4,7},{5,6},{6,5},{7,4},{8,11},{9,10},{10,... | collective-permute-start | bytes 196616 | tf_op jit(solution)/shard_map/ppermute | solution.py:586
  18.8 0.9 %copy-start = (f32[400,128]{1,0:T(8,128)S(1)}, f32[400,128]{1,0:T(8,128)}, u32[]{:S(2)}) copy-start(f32[400,128]{1,0:T(8,128)} %get-tuple-element.17.refs_0_) | copy-start | bytes 614404

commit v3 on v2

--- a/solution.py
+++ b/solution.py
@@ -474,8 +474,11 @@
             low = jnp.where(first_own, rows[0], rows[1])
             high = jnp.where(third_own, rows[2], rows[3])
             sources.append(jnp.where(lower_half, low, high))
-        dist_ref[...] = jnp.dot(jnp.concatenate(sources, axis=0), targets, preferred_element_type=F32)
-        yield
+            if j % 4 == 3:
+                rows = pl.ds(LEAF * (j - 3), 4 * LEAF)
+                dist_ref[rows, :] = jnp.dot(jnp.concatenate(sources, axis=0), targets, preferred_element_type=F32)
+                sources = []
+                yield
 
     def pull(quad, slot_ref, dist_ref):
         total = jnp.zeros((4 * M_ROWS, 256), F32)
@@ -494,16 +497,10 @@
             out_ref[:, lanes] = out_ref[:, lanes] + point_sums(sums, pair_place(tg_ref, pair))
 
     quads, octets = LEAF_DEV // 4, LEAF_DEV // 8
+    run(build(0))
     copy.wait()
-    first, moments, distance = build(0), features(0, 0, even_ref), distances(0, dist_even)
-    for step in range(4):
-        run(first, 8)
-        run(moments, 1)
-        if step % 2 == 0:
-            run(distance, 1)
-    run(first)
-    run(moments)
-    run(distance)
+    run(features(0, 0, even_ref))
+    run(distances(0, dist_even))
 
     def one_octet(octet, carry):
         quad = 2 * octet
@@ -519,7 +516,7 @@
             direct = pull(now, slot_ref, dist_ref)
             moments, distance = features(ahead, raw_at, ahead_slot), distances(ahead, ahead_dist)
             for step in range(8):
-                if step == 1:
+                if step % 2 == 1:
                     run(distance, 1)
                 run(direct, 1)
                 if step % 2 == 0:

time: 49 us -> 47.4 us (0.967)
  Pallas kernels: 31.3 us -> 29.7 us
    pallas_call x1, Pallas kernels: 24.6 us -> 23 us  [on_device(): pl.pallas_call(functools.partial(pull_kernel, n_dom, n_sub), out_shape=ja...]
where the time goes in v3:
time: 47.4 us; the launch traced here: 47.2 us
  Pallas kernels  29.7 us (63%)
  starting transfers between devices  10.6 us (22%)
  waiting for transfers between devices  5.83 us (12%)
  local copies, waits for them, and re-layouts  0.93 us (2%)
    pallas_call x1, Pallas kernels, on_device(): pl.pallas_call(functools.partial(pull_kernel, n_dom, n_sub), out_shape=ja...  23 us
    all_to_all x1, starting transfers between devices, on_device(): lax.all_to_all(sent, 'dom', split_axis=0, concat_axis=0, tiled=True)  7.26 us
    pallas_call x1, Pallas kernels, on_device(): pl.pallas_call(functools.partial(prepare_kernel, n_dom, n_sub), out_shape...  4.46 us
    ppermute x6, waiting for transfers between devices, across(): lax.ppermute(value, 'sub', [(seg, seg ^ bits) for seg in range(n_sub)])  3.67 us
    ppermute x6, starting transfers between devices, across(): lax.ppermute(value, 'sub', [(seg, seg ^ bits) for seg in range(n_sub)])  3.38 us
    pallas_call x1, Pallas kernels, on_device(): pl.pallas_call(functools.partial(pack_kernel, n_dom), out_shape=(jax.Shap...  2.29 us
    all_to_all x1, waiting for transfers between devices, on_device(): lax.all_to_all(sent, 'dom', split_axis=0, concat_axis=0, tiled=True)  2.16 us
  transfers between devices with their start and end apart: 7, of which 2 were waited for; matrix products, arithmetic and copies ran while one was open for 0% of the time, Pallas kernels for 9%

profile of v3, /device:TPU:0, one launch (start us, length us, event | category | flops | bytes accessed | tf_op | source)
XLA Modules:
  0.0 47.2 jit_solution(6522991787846471398)
XLA Ops:
  0.0 2.3 %pack_own.1 = (f32[256,128]{1,0:T(8,128)}, f32[8,32,128]{2,1,0:T(8,128)}, f32[400,128]{1,0:T(8,128)}) custom-call(f32[3,8192]{1,0:T(4,128)} %refs_0_.1, f32[1,8192]{1,0:T(1,128)} %bitcast.5, f32[1,128]{1,0:T(1,128)} %bitcast.8, f32[3,128]{1,0:T(4,128)} %refs_3_.1, f32[6,128]{1,0:T(8,128)} %refs_4_.1, s32[128,128]{1,0:T(8,128)} %refs_5_.1, ...), custom_call_target="tpu_custom_call" | custom-call | tf_op jit(solution)/shard_map/pack_own/pallas_call | solution.py:561
  2.3 7.3 %all-to-all-start = ((f32[8,32,128]{2,1,0:T(8,128)}), f32[8,32,128]{2,1,0:T(8,128)S(1)}, u32[]{:S(2)}, u32[]{:S(2)}) async-start(f32[8,32,128]{2,1,0:T(8,128)} %get-tuple-element.16), calls=%async_computation | async-start | bytes 262144 | tf_op jit(solution)/shard_map/all_to_all | solution.py:580
  9.6 1.5 %collective-permute-start.4 = (f32[256,128]{1,0:T(8,128)}, f32[256,128]{1,0:T(8,128)S(1)}, u32[]{:S(2)}, u32[]{:S(2)}) collective-permute-start(f32[256,128]{1,0:T(8,128)} %get-tuple-element.18), channel_id=1, source_target_pairs={{0,2},{1,3},{2,0},{3,1},{4,6},{5,7},{6,4},{7,5},{8,10},{9,11},{10,... | collective-permute-start | bytes 393224 | tf_op jit(solution)/shard_map/ppermute | solution.py:583
  11.1 0.0 collective-permute-start.3
  11.1 3.7 %collective-permute-done.4.refs_2_ = f32[256,128]{1,0:T(8,128)S(1)} collective-permute-done((f32[256,128]{1,0:T(8,128)}, f32[256,128]{1,0:T(8,128)S(1)}, u32[]{:S(2)}, u32[]{:S(2)}) %collective-permute-start.4) | collective-permute-done | bytes 131104 | tf_op jit(solution)/shard_map/ppermute | solution.py:583
  14.7 0.0 collective-permute-start.5
  14.7 2.2 %all-to-all-done.refs_4_ = f32[8,32,128]{2,1,0:T(8,128)S(1)} async-done(((f32[8,32,128]{2,1,0:T(8,128)}), f32[8,32,128]{2,1,0:T(8,128)S(1)}, u32[]{:S(2)}, u32[]{:S(2)}) %all-to-all-start) | async-done | bytes 131104 | tf_op jit(solution)/shard_map/all_to_all | solution.py:580
  16.9 0.0 collective-permute-start
  16.9 1.6 %collective-permute-start.1 = (f32[8,16,128]{2,1,0:T(8,128)S(1)}, f32[8,16,128]{2,1,0:T(8,128)S(1)}, u32[]{:S(2)}, u32[]{:S(2)}) collective-permute-start(f32[8,16,128]{2,1,0:T(8,128)S(1)} %slice.4.refs_0_), channel_id=1, source_target_pairs={{0,2},{1,3},{2,0},{3,1},{4,6},{5,7},{6,4},{7,5},{8,10},{9,11},{10,... | collective-permute-start | bytes 196616 | tf_op jit(solution)/shard_map/ppermute | solution.py:583
  18.5 0.3 collective-permute-start.2
  18.8 0.0 collective-permute-done.3.refs_1_
  18.8 0.0 collective-permute-done.5.refs_3_
  18.8 0.0 copy-start
  18.8 0.9 %copy-done = f32[400,128]{1,0:T(8,128)S(1)} copy-done((f32[400,128]{1,0:T(8,128)S(1)}, f32[400,128]{1,0:T(8,128)}, u32[]{:S(2)}) %copy-start) | copy-done | bytes 204824
  19.7 4.5 %prepare.1 = (f32[576,4,128]{2,1,0:T(4,128)S(1)}, bf16[576,64,128]{2,1,0:T(8,128)(2,1)S(1)}, bf16[64,32,128]{2,1,0:T(8,128)(2,1)S(1)}, f32[256,128]{1,0:T(8,128)...) custom-call(f32[400,128]{1,0:T(8,128)S(1)} %copy-done, ...), custom_call_target="tpu_custom_call" | custom-call | bytes 20000000 | tf_op jit(solution)/shard_map/prepare/pallas_call | solution.py:594
  24.2 0.0 collective-permute-done.refs_1_
  24.2 0.0 collective-permute-done.1.refs_2_
  24.2 0.0 collective-permute-done.2.refs_3_
  24.2 23.0 %pull.1 = f32[3,8192]{1,0:T(4,128)} custom-call(f32[8,16,128]{2,1,0:T(8,128)S(1)} %slice.4.refs_0_, f32[8,16,128]{2,1,0:T(8,128)S(1)} %collective-permute-done.refs_1_, f32[8,16,128]{2,1,0:T(8,128)S(1)} %collective-permute-done.1.refs_2_, f32[8,16,128]{2,1,0:T(8,128)S(1)} %collective-permute-done.2.refs_3_, f32[576,4,128]{2,1,0:T(4,128)S(1)} %get-tuple-element.19.refs_4_, ...), custom_call_target="tpu_custom_call" | custom-call | tf_op jit(solution)/shard_map/pull/pallas_call | solution.py:616
  (1 shorter events, 0.0 us)
Async XLA Ops:
  2.3 14.6 %all-to-all-start = ((f32[8,32,128]{2,1,0:T(8,128)}), f32[8,32,128]{2,1,0:T(8,128)S(1)}, u32[]{:S(2)}, u32[]{:S(2)}) async-start(f32[8,32,128]{2,1,0:T(8,128)} %get-tuple-element.16), calls=%async_computation | async-start | bytes 262144 | tf_op jit(solution)/shard_map/all_to_all | solution.py:580
  9.6 5.2 %collective-permute-start.4 = (f32[256,128]{1,0:T(8,128)}, f32[256,128]{1,0:T(8,128)S(1)}, u32[]{:S(2)}, u32[]{:S(2)}) collective-permute-start(f32[256,128]{1,0:T(8,128)} %get-tuple-element.18), channel_id=1, source_target_pairs={{0,2},{1,3},{2,0},{3,1},{4,6},{5,7},{6,4},{7,5},{8,10},{9,11},{10,... | collective-permute-start | bytes 393224 | tf_op jit(solution)/shard_map/ppermute | solution.py:583
  11.1 7.7 %collective-permute-start.3 = (f32[256,128]{1,0:T(8,128)}, f32[256,128]{1,0:T(8,128)S(1)}, u32[]{:S(2)}, u32[]{:S(2)}) collective-permute-start(f32[256,128]{1,0:T(8,128)} %get-tuple-element.18), channel_id=1, source_target_pairs={{0,1},{1,0},{2,3},{3,2},{4,5},{5,4},{6,7},{7,6},{8,9},{9,8},{10,11... | collective-permute-start | bytes 393224 | tf_op jit(solution)/shard_map/ppermute | solution.py:583
  14.7 4.0 %collective-permute-start.5 = (f32[256,128]{1,0:T(8,128)S(1)}, f32[256,128]{1,0:T(8,128)S(1)}, u32[]{:S(2)}, u32[]{:S(2)}) collective-permute-start(f32[256,128]{1,0:T(8,128)S(1)} %collective-permute-done.4.refs_2_), channel_id=1, source_target_pairs={{0,1},{1,0},{2,3},{3,2},{4,5},{5,4},{6,7},{7,6},{8,9},{9,8},{10,11... | collective-permute-start | bytes 393224 | tf_op jit(solution)/shard_map/ppermute | solution.py:583
  16.9 7.3 %collective-permute-start = (f32[8,16,128]{2,1,0:T(8,128)S(1)}, f32[8,16,128]{2,1,0:T(8,128)S(1)}, u32[]{:S(2)}, u32[]{:S(2)}) collective-permute-start(f32[8,16,128]{2,1,0:T(8,128)S(1)} %slice.4.refs_0_), channel_id=1, source_target_pairs={{0,1},{1,0},{2,3},{3,2},{4,5},{5,4},{6,7},{7,6},{8,9},{9,8},{10,11... | collective-permute-start | bytes 196616 | tf_op jit(solution)/shard_map/ppermute | solution.py:583
  16.9 7.3 %collective-permute-start.1 = (f32[8,16,128]{2,1,0:T(8,128)S(1)}, f32[8,16,128]{2,1,0:T(8,128)S(1)}, u32[]{:S(2)}, u32[]{:S(2)}) collective-permute-start(f32[8,16,128]{2,1,0:T(8,128)S(1)} %slice.4.refs_0_), channel_id=1, source_target_pairs={{0,2},{1,3},{2,0},{3,1},{4,6},{5,7},{6,4},{7,5},{8,10},{9,11},{10,... | collective-permute-start | bytes 196616 | tf_op jit(solution)/shard_map/ppermute | solution.py:583
  18.5 5.7 %collective-permute-start.2 = (f32[8,16,128]{2,1,0:T(8,128)S(1)}, f32[8,16,128]{2,1,0:T(8,128)S(1)}, u32[]{:S(2)}, u32[]{:S(2)}) collective-permute-start(f32[8,16,128]{2,1,0:T(8,128)S(1)} %slice.4.refs_0_), channel_id=1, source_target_pairs={{0,3},{1,2},{2,1},{3,0},{4,7},{5,6},{6,5},{7,4},{8,11},{9,10},{10,... | collective-permute-start | bytes 196616 | tf_op jit(solution)/shard_map/ppermute | solution.py:583
  18.8 0.9 %copy-start = (f32[400,128]{1,0:T(8,128)S(1)}, f32[400,128]{1,0:T(8,128)}, u32[]{:S(2)}) copy-start(f32[400,128]{1,0:T(8,128)} %get-tuple-element.17.refs_0_) | copy-start | bytes 614404

commit v4 on v3

--- a/solution.py
+++ b/solution.py
@@ -284,6 +284,7 @@
         axis=0,
     )
     forms = jnp.dot(target[:, 0 : H_ROWS + Q_ROWS], forms, preferred_element_type=F32)
+    yield
     dist_sq, quad_form = forms[:, 0:128], forms[:, 128:256]
     inv = lax.rsqrt(dist_sq)
     inv_two = inv * inv
@@ -296,8 +297,7 @@
         ],
         axis=0,
     )
-    both = jnp.concatenate([stacked(pull), stacked(inv_three * inv_two)], axis=1)
-    return both, moments
+    return jnp.concatenate([stacked(pull), stacked(inv_three * inv_two)], axis=1), moments
 
 
 def pair_lanes(pair):
@@ -318,9 +318,9 @@
     left = lax.broadcasted_iota(jnp.int32, (LEAF, 128), 1) < LEAF
     for inner in range(4):
         pair = octet * 4 + inner
-        first, first_moments = cell_group(2 * inner, ah_ref[pair, 0:LEAF, :], cf_ref, cm_ref)
+        first, first_moments = yield from cell_group(2 * inner, ah_ref[pair, 0:LEAF, :], cf_ref, cm_ref)
+        second, second_moments = yield from cell_group(2 * inner + 1, ah_ref[pair, LEAF:, :], cf_ref, cm_ref)
         yield
-        second, second_moments = cell_group(2 * inner + 1, ah_ref[pair, LEAF:, :], cf_ref, cm_ref)
         moments = jnp.concatenate([first_moments, second_moments], axis=0)
         sums = transposed_dot(jnp.concatenate([first, second], axis=0), moments)
         yield
@@ -523,10 +523,7 @@
                     run(moments, 1)
                 if half == 0 or step < 4:
                     run(coming, 3)
-                    if step % 4 != 3:
-                        run(cells, 1)
-                elif step == 4:
-                    run(cells)
+                    run(cells, 2 if half or step % 2 else 1)
                 else:
                     run(coming, 1)
             run(moments)

time: 47.4 us -> 47.1 us (level)
  transfers between devices with their start and end apart: 7 -> 7, of which waited for: 2 -> 2; matrix products, arithmetic and copies ran while one was open for 0% -> 0% of each run, Pallas kernels for 9% -> 10%
where the time goes in v4:
time: 47.1 us; the launch traced here: 46.8 us
  Pallas kernels  29.3 us (62%)
  starting transfers between devices  10.6 us (23%)
  waiting for transfers between devices  5.83 us (12%)
  local copies, waits for them, and re-layouts  0.93 us (2%)
    pallas_call x1, Pallas kernels, on_device(): pl.pallas_call(functools.partial(pull_kernel, n_dom, n_sub), out_shape=ja...  22.6 us
    all_to_all x1, starting transfers between devices, on_device(): lax.all_to_all(sent, 'dom', split_axis=0, concat_axis=0, tiled=True)  7.26 us
    pallas_call x1, Pallas kernels, on_device(): pl.pallas_call(functools.partial(prepare_kernel, n_dom, n_sub), out_shape...  4.46 us
    ppermute x6, waiting for transfers between devices, across(): lax.ppermute(value, 'sub', [(seg, seg ^ bits) for seg in range(n_sub)])  3.67 us
    ppermute x6, starting transfers between devices, across(): lax.ppermute(value, 'sub', [(seg, seg ^ bits) for seg in range(n_sub)])  3.38 us
    pallas_call x1, Pallas kernels, on_device(): pl.pallas_call(functools.partial(pack_kernel, n_dom), out_shape=(jax.Shap...  2.29 us
    all_to_all x1, waiting for transfers between devices, on_device(): lax.all_to_all(sent, 'dom', split_axis=0, concat_axis=0, tiled=True)  2.16 us
  transfers between devices with their start and end apart: 7, of which 2 were waited for; matrix products, arithmetic and copies ran while one was open for 0% of the time, Pallas kernels for 10%

profile of v4, /device:TPU:0, one launch (start us, length us, event | category | flops | bytes accessed | tf_op | source)
XLA Modules:
  0.0 46.8 jit_solution(13752455746725065837)
XLA Ops:
  0.0 2.3 %pack_own.1 = (f32[256,128]{1,0:T(8,128)}, f32[8,32,128]{2,1,0:T(8,128)}, f32[400,128]{1,0:T(8,128)}) custom-call(f32[3,8192]{1,0:T(4,128)} %refs_0_.1, f32[1,8192]{1,0:T(1,128)} %bitcast.5, f32[1,128]{1,0:T(1,128)} %bitcast.8, f32[3,128]{1,0:T(4,128)} %refs_3_.1, f32[6,128]{1,0:T(8,128)} %refs_4_.1, s32[128,128]{1,0:T(8,128)} %refs_5_.1, ...), custom_call_target="tpu_custom_call" | custom-call | tf_op jit(solution)/shard_map/pack_own/pallas_call | solution.py:558
  2.3 7.3 %all-to-all-start = ((f32[8,32,128]{2,1,0:T(8,128)}), f32[8,32,128]{2,1,0:T(8,128)S(1)}, u32[]{:S(2)}, u32[]{:S(2)}) async-start(f32[8,32,128]{2,1,0:T(8,128)} %get-tuple-element.16), calls=%async_computation | async-start | bytes 262144 | tf_op jit(solution)/shard_map/all_to_all | solution.py:577
  9.6 1.5 %collective-permute-start.4 = (f32[256,128]{1,0:T(8,128)}, f32[256,128]{1,0:T(8,128)S(1)}, u32[]{:S(2)}, u32[]{:S(2)}) collective-permute-start(f32[256,128]{1,0:T(8,128)} %get-tuple-element.18), channel_id=1, source_target_pairs={{0,2},{1,3},{2,0},{3,1},{4,6},{5,7},{6,4},{7,5},{8,10},{9,11},{10,... | collective-permute-start | bytes 393224 | tf_op jit(solution)/shard_map/ppermute | solution.py:580
  11.1 0.0 collective-permute-start.3
  11.1 3.7 %collective-permute-done.4.refs_2_ = f32[256,128]{1,0:T(8,128)S(1)} collective-permute-done((f32[256,128]{1,0:T(8,128)}, f32[256,128]{1,0:T(8,128)S(1)}, u32[]{:S(2)}, u32[]{:S(2)}) %collective-permute-start.4) | collective-permute-done | bytes 131104 | tf_op jit(solution)/shard_map/ppermute | solution.py:580
  14.7 0.0 collective-permute-start.5
  14.7 2.2 %all-to-all-done.refs_4_ = f32[8,32,128]{2,1,0:T(8,128)S(1)} async-done(((f32[8,32,128]{2,1,0:T(8,128)}), f32[8,32,128]{2,1,0:T(8,128)S(1)}, u32[]{:S(2)}, u32[]{:S(2)}) %all-to-all-start) | async-done | bytes 131104 | tf_op jit(solution)/shard_map/all_to_all | solution.py:577
  16.9 0.0 collective-permute-start
  16.9 1.6 %collective-permute-start.1 = (f32[8,16,128]{2,1,0:T(8,128)S(1)}, f32[8,16,128]{2,1,0:T(8,128)S(1)}, u32[]{:S(2)}, u32[]{:S(2)}) collective-permute-start(f32[8,16,128]{2,1,0:T(8,128)S(1)} %slice.4.refs_0_), channel_id=1, source_target_pairs={{0,2},{1,3},{2,0},{3,1},{4,6},{5,7},{6,4},{7,5},{8,10},{9,11},{10,... | collective-permute-start | bytes 196616 | tf_op jit(solution)/shard_map/ppermute | solution.py:580
  18.5 0.3 collective-permute-start.2
  18.8 0.0 collective-permute-done.3.refs_1_
  18.8 0.0 collective-permute-done.5.refs_3_
  18.8 0.0 copy-start
  18.8 0.9 %copy-done = f32[400,128]{1,0:T(8,128)S(1)} copy-done((f32[400,128]{1,0:T(8,128)S(1)}, f32[400,128]{1,0:T(8,128)}, u32[]{:S(2)}) %copy-start) | copy-done | bytes 204824
  19.7 4.5 %prepare.1 = (f32[576,4,128]{2,1,0:T(4,128)S(1)}, bf16[576,64,128]{2,1,0:T(8,128)(2,1)S(1)}, bf16[64,32,128]{2,1,0:T(8,128)(2,1)S(1)}, f32[256,128]{1,0:T(8,128)...) custom-call(f32[400,128]{1,0:T(8,128)S(1)} %copy-done, ...), custom_call_target="tpu_custom_call" | custom-call | bytes 20000000 | tf_op jit(solution)/shard_map/prepare/pallas_call | solution.py:591
  24.2 0.0 collective-permute-done.refs_1_
  24.2 0.0 collective-permute-done.1.refs_2_
  24.2 0.0 collective-permute-done.2.refs_3_
  24.2 22.6 %pull.1 = f32[3,8192]{1,0:T(4,128)} custom-call(f32[8,16,128]{2,1,0:T(8,128)S(1)} %slice.4.refs_0_, f32[8,16,128]{2,1,0:T(8,128)S(1)} %collective-permute-done.refs_1_, f32[8,16,128]{2,1,0:T(8,128)S(1)} %collective-permute-done.1.refs_2_, f32[8,16,128]{2,1,0:T(8,128)S(1)} %collective-permute-done.2.refs_3_, f32[576,4,128]{2,1,0:T(4,128)S(1)} %get-tuple-element.19.refs_4_, ...), custom_call_target="tpu_custom_call" | custom-call | tf_op jit(solution)/shard_map/pull/pallas_call | solution.py:613
  (1 shorter events, 0.0 us)
Async XLA Ops:
  2.3 14.6 %all-to-all-start = ((f32[8,32,128]{2,1,0:T(8,128)}), f32[8,32,128]{2,1,0:T(8,128)S(1)}, u32[]{:S(2)}, u32[]{:S(2)}) async-start(f32[8,32,128]{2,1,0:T(8,128)} %get-tuple-element.16), calls=%async_computation | async-start | bytes 262144 | tf_op jit(solution)/shard_map/all_to_all | solution.py:577
  9.6 5.2 %collective-permute-start.4 = (f32[256,128]{1,0:T(8,128)}, f32[256,128]{1,0:T(8,128)S(1)}, u32[]{:S(2)}, u32[]{:S(2)}) collective-permute-start(f32[256,128]{1,0:T(8,128)} %get-tuple-element.18), channel_id=1, source_target_pairs={{0,2},{1,3},{2,0},{3,1},{4,6},{5,7},{6,4},{7,5},{8,10},{9,11},{10,... | collective-permute-start | bytes 393224 | tf_op jit(solution)/shard_map/ppermute | solution.py:580
  11.1 7.7 %collective-permute-start.3 = (f32[256,128]{1,0:T(8,128)}, f32[256,128]{1,0:T(8,128)S(1)}, u32[]{:S(2)}, u32[]{:S(2)}) collective-permute-start(f32[256,128]{1,0:T(8,128)} %get-tuple-element.18), channel_id=1, source_target_pairs={{0,1},{1,0},{2,3},{3,2},{4,5},{5,4},{6,7},{7,6},{8,9},{9,8},{10,11... | collective-permute-start | bytes 393224 | tf_op jit(solution)/shard_map/ppermute | solution.py:580
  14.7 4.0 %collective-permute-start.5 = (f32[256,128]{1,0:T(8,128)S(1)}, f32[256,128]{1,0:T(8,128)S(1)}, u32[]{:S(2)}, u32[]{:S(2)}) collective-permute-start(f32[256,128]{1,0:T(8,128)S(1)} %collective-permute-done.4.refs_2_), channel_id=1, source_target_pairs={{0,1},{1,0},{2,3},{3,2},{4,5},{5,4},{6,7},{7,6},{8,9},{9,8},{10,11... | collective-permute-start | bytes 393224 | tf_op jit(solution)/shard_map/ppermute | solution.py:580
  16.9 7.3 %collective-permute-start = (f32[8,16,128]{2,1,0:T(8,128)S(1)}, f32[8,16,128]{2,1,0:T(8,128)S(1)}, u32[]{:S(2)}, u32[]{:S(2)}) collective-permute-start(f32[8,16,128]{2,1,0:T(8,128)S(1)} %slice.4.refs_0_), channel_id=1, source_target_pairs={{0,1},{1,0},{2,3},{3,2},{4,5},{5,4},{6,7},{7,6},{8,9},{9,8},{10,11... | collective-permute-start | bytes 196616 | tf_op jit(solution)/shard_map/ppermute | solution.py:580
  16.9 7.3 %collective-permute-start.1 = (f32[8,16,128]{2,1,0:T(8,128)S(1)}, f32[8,16,128]{2,1,0:T(8,128)S(1)}, u32[]{:S(2)}, u32[]{:S(2)}) collective-permute-start(f32[8,16,128]{2,1,0:T(8,128)S(1)} %slice.4.refs_0_), channel_id=1, source_target_pairs={{0,2},{1,3},{2,0},{3,1},{4,6},{5,7},{6,4},{7,5},{8,10},{9,11},{10,... | collective-permute-start | bytes 196616 | tf_op jit(solution)/shard_map/ppermute | solution.py:580
  18.5 5.7 %collective-permute-start.2 = (f32[8,16,128]{2,1,0:T(8,128)S(1)}, f32[8,16,128]{2,1,0:T(8,128)S(1)}, u32[]{:S(2)}, u32[]{:S(2)}) collective-permute-start(f32[8,16,128]{2,1,0:T(8,128)S(1)} %slice.4.refs_0_), channel_id=1, source_target_pairs={{0,3},{1,2},{2,1},{3,0},{4,7},{5,6},{6,5},{7,4},{8,11},{9,10},{10,... | collective-permute-start | bytes 196616 | tf_op jit(solution)/shard_map/ppermute | solution.py:580
  18.8 0.9 %copy-start = (f32[400,128]{1,0:T(8,128)S(1)}, f32[400,128]{1,0:T(8,128)}, u32[]{:S(2)}) copy-start(f32[400,128]{1,0:T(8,128)} %get-tuple-element.17.refs_0_) | copy-start | bytes 614404

commit v5 on v4

--- a/solution.py
+++ b/solution.py
@@ -481,18 +481,18 @@
                 yield
 
     def pull(quad, slot_ref, dist_ref):
-        total = jnp.zeros((4 * M_ROWS, 256), F32)
+        totals = [jnp.zeros((2 * M_ROWS, 128), F32) for _ in range(2)]
         for chunk in range(8):
-            inv = lax.rsqrt(dist_ref[128 * chunk : 128 * chunk + 128, :])
-            weights = stacked(inv * inv * inv)
-            rows = [slot_ref[group, pl.ds(chunk, M_ROWS, stride=8), :] for group in range(4)]
-            rows = jnp.concatenate(rows, axis=0).astype(BF16)
-            total += jnp.dot(jnp.concatenate([rows, rows], axis=1), weights, preferred_element_type=F32)
-            yield
+            for side in range(2):
+                inv = lax.rsqrt(dist_ref[128 * chunk : 128 * chunk + 128, 128 * side : 128 * side + 128])
+                weights = stacked(inv * inv * inv)
+                rows = [slot_ref[2 * side + half, pl.ds(chunk, M_ROWS, stride=8), :] for half in range(2)]
+                rows = jnp.concatenate(rows, axis=0).astype(BF16)
+                totals[side] += jnp.dot(jnp.concatenate([rows, rows], axis=1), weights, preferred_element_type=F32)
+                yield
         for side in range(2):
             pair = 2 * quad + side
-            at, columns = 2 * M_ROWS * side, slice(128 * side, 128 * side + 128)
-            sums = jnp.where(left, total[at : at + M_ROWS, columns], total[at + M_ROWS : at + 2 * M_ROWS, columns])
+            sums = jnp.where(left, totals[side][0:M_ROWS], totals[side][M_ROWS:])
             lanes = pair_lanes(pair)
             out_ref[:, lanes] = out_ref[:, lanes] + point_sums(sums, pair_place(tg_ref, pair))
 
@@ -526,6 +526,7 @@
                     run(cells, 2 if half or step % 2 else 1)
                 else:
                     run(coming, 1)
+                run(direct, 1)
             run(moments)
             run(distance)
             run(direct)

time: 47.1 us -> 45.5 us (0.966)
  Pallas kernels: 29.3 us -> 27.7 us
    pallas_call x1, Pallas kernels: 22.6 us -> 21 us  [on_device(): pl.pallas_call(functools.partial(pull_kernel, n_dom, n_sub), out_shape=ja...]
where the time goes in v5:
time: 45.5 us; the launch traced here: 45.2 us
  Pallas kernels  27.7 us (61%)
  starting transfers between devices  10.6 us (23%)
  waiting for transfers between devices  5.83 us (13%)
  local copies, waits for them, and re-layouts  0.93 us (2%)
    pallas_call x1, Pallas kernels, on_device(): pl.pallas_call(functools.partial(pull_kernel, n_dom, n_sub), out_shape=ja...  21 us
    all_to_all x1, starting transfers between devices, on_device(): lax.all_to_all(sent, 'dom', split_axis=0, concat_axis=0, tiled=True)  7.26 us
    pallas_call x1, Pallas kernels, on_device(): pl.pallas_call(functools.partial(prepare_kernel, n_dom, n_sub), out_shape...  4.46 us
    ppermute x6, waiting for transfers between devices, across(): lax.ppermute(value, 'sub', [(seg, seg ^ bits) for seg in range(n_sub)])  3.67 us
    ppermute x6, starting transfers between devices, across(): lax.ppermute(value, 'sub', [(seg, seg ^ bits) for seg in range(n_sub)])  3.38 us
    pallas_call x1, Pallas kernels, on_device(): pl.pallas_call(functools.partial(pack_kernel, n_dom), out_shape=(jax.Shap...  2.29 us
    all_to_all x1, waiting for transfers between devices, on_device(): lax.all_to_all(sent, 'dom', split_axis=0, concat_axis=0, tiled=True)  2.16 us
    unnamed x2, local copies, waits for them, and re-layouts  0.93 us
  transfers between devices with their start and end apart: 7, of which 2 were waited for; matrix products, arithmetic and copies ran while one was open for 0% of the time, Pallas kernels for 10%

profile of v5, /device:TPU:0, one launch (start us, length us, event | category | flops | bytes accessed | tf_op | source)
XLA Modules:
  0.0 45.2 jit_solution(14320662019133397657)
XLA Ops:
  0.0 2.3 %pack_own.1 = (f32[256,128]{1,0:T(8,128)}, f32[8,32,128]{2,1,0:T(8,128)}, f32[400,128]{1,0:T(8,128)}) custom-call(f32[3,8192]{1,0:T(4,128)} %refs_0_.1, f32[1,8192]{1,0:T(1,128)} %bitcast.5, f32[1,128]{1,0:T(1,128)} %bitcast.8, f32[3,128]{1,0:T(4,128)} %refs_3_.1, f32[6,128]{1,0:T(8,128)} %refs_4_.1, s32[128,128]{1,0:T(8,128)} %refs_5_.1, ...), custom_call_target="tpu_custom_call" | custom-call | tf_op jit(solution)/shard_map/pack_own/pallas_call | solution.py:559
  2.3 7.3 %all-to-all-start = ((f32[8,32,128]{2,1,0:T(8,128)}), f32[8,32,128]{2,1,0:T(8,128)S(1)}, u32[]{:S(2)}, u32[]{:S(2)}) async-start(f32[8,32,128]{2,1,0:T(8,128)} %get-tuple-element.16), calls=%async_computation | async-start | bytes 262144 | tf_op jit(solution)/shard_map/all_to_all | solution.py:578
  9.6 1.5 %collective-permute-start.4 = (f32[256,128]{1,0:T(8,128)}, f32[256,128]{1,0:T(8,128)S(1)}, u32[]{:S(2)}, u32[]{:S(2)}) collective-permute-start(f32[256,128]{1,0:T(8,128)} %get-tuple-element.18), channel_id=1, source_target_pairs={{0,2},{1,3},{2,0},{3,1},{4,6},{5,7},{6,4},{7,5},{8,10},{9,11},{10,... | collective-permute-start | bytes 393224 | tf_op jit(solution)/shard_map/ppermute | solution.py:581
  11.1 0.0 collective-permute-start.3
  11.1 3.7 %collective-permute-done.4.refs_2_ = f32[256,128]{1,0:T(8,128)S(1)} collective-permute-done((f32[256,128]{1,0:T(8,128)}, f32[256,128]{1,0:T(8,128)S(1)}, u32[]{:S(2)}, u32[]{:S(2)}) %collective-permute-start.4) | collective-permute-done | bytes 131104 | tf_op jit(solution)/shard_map/ppermute | solution.py:581
  14.7 0.0 collective-permute-start.5
  14.7 2.2 %all-to-all-done.refs_4_ = f32[8,32,128]{2,1,0:T(8,128)S(1)} async-done(((f32[8,32,128]{2,1,0:T(8,128)}), f32[8,32,128]{2,1,0:T(8,128)S(1)}, u32[]{:S(2)}, u32[]{:S(2)}) %all-to-all-start) | async-done | bytes 131104 | tf_op jit(solution)/shard_map/all_to_all | solution.py:578
  16.9 0.0 collective-permute-start
  16.9 1.6 %collective-permute-start.1 = (f32[8,16,128]{2,1,0:T(8,128)S(1)}, f32[8,16,128]{2,1,0:T(8,128)S(1)}, u32[]{:S(2)}, u32[]{:S(2)}) collective-permute-start(f32[8,16,128]{2,1,0:T(8,128)S(1)} %slice.4.refs_0_), channel_id=1, source_target_pairs={{0,2},{1,3},{2,0},{3,1},{4,6},{5,7},{6,4},{7,5},{8,10},{9,11},{10,... | collective-permute-start | bytes 196616 | tf_op jit(solution)/shard_map/ppermute | solution.py:581
  18.5 0.3 collective-permute-start.2
  18.8 0.0 collective-permute-done.3.refs_1_
  18.8 0.0 collective-permute-done.5.refs_3_
  18.8 0.0 copy-start
  18.8 0.9 %copy-done = f32[400,128]{1,0:T(8,128)S(1)} copy-done((f32[400,128]{1,0:T(8,128)S(1)}, f32[400,128]{1,0:T(8,128)}, u32[]{:S(2)}) %copy-start) | copy-done | bytes 204824
  19.7 4.5 %prepare.1 = (f32[576,4,128]{2,1,0:T(4,128)S(1)}, bf16[576,64,128]{2,1,0:T(8,128)(2,1)S(1)}, bf16[64,32,128]{2,1,0:T(8,128)(2,1)S(1)}, f32[256,128]{1,0:T(8,128)...) custom-call(f32[400,128]{1,0:T(8,128)S(1)} %copy-done, ...), custom_call_target="tpu_custom_call" | custom-call | bytes 20000000 | tf_op jit(solution)/shard_map/prepare/pallas_call | solution.py:592
  24.2 0.0 collective-permute-done.refs_1_
  24.2 0.0 collective-permute-done.1.refs_2_
  24.2 0.0 collective-permute-done.2.refs_3_
  24.2 21.0 %pull.1 = f32[3,8192]{1,0:T(4,128)} custom-call(f32[8,16,128]{2,1,0:T(8,128)S(1)} %slice.4.refs_0_, f32[8,16,128]{2,1,0:T(8,128)S(1)} %collective-permute-done.refs_1_, f32[8,16,128]{2,1,0:T(8,128)S(1)} %collective-permute-done.1.refs_2_, f32[8,16,128]{2,1,0:T(8,128)S(1)} %collective-permute-done.2.refs_3_, f32[576,4,128]{2,1,0:T(4,128)S(1)} %get-tuple-element.19.refs_4_, ...), custom_call_target="tpu_custom_call" | custom-call | tf_op jit(solution)/shard_map/pull/pallas_call | solution.py:614
  (1 shorter events, 0.0 us)
Async XLA Ops:
  2.3 14.6 %all-to-all-start = ((f32[8,32,128]{2,1,0:T(8,128)}), f32[8,32,128]{2,1,0:T(8,128)S(1)}, u32[]{:S(2)}, u32[]{:S(2)}) async-start(f32[8,32,128]{2,1,0:T(8,128)} %get-tuple-element.16), calls=%async_computation | async-start | bytes 262144 | tf_op jit(solution)/shard_map/all_to_all | solution.py:578
  9.6 5.2 %collective-permute-start.4 = (f32[256,128]{1,0:T(8,128)}, f32[256,128]{1,0:T(8,128)S(1)}, u32[]{:S(2)}, u32[]{:S(2)}) collective-permute-start(f32[256,128]{1,0:T(8,128)} %get-tuple-element.18), channel_id=1, source_target_pairs={{0,2},{1,3},{2,0},{3,1},{4,6},{5,7},{6,4},{7,5},{8,10},{9,11},{10,... | collective-permute-start | bytes 393224 | tf_op jit(solution)/shard_map/ppermute | solution.py:581
  11.1 7.7 %collective-permute-start.3 = (f32[256,128]{1,0:T(8,128)}, f32[256,128]{1,0:T(8,128)S(1)}, u32[]{:S(2)}, u32[]{:S(2)}) collective-permute-start(f32[256,128]{1,0:T(8,128)} %get-tuple-element.18), channel_id=1, source_target_pairs={{0,1},{1,0},{2,3},{3,2},{4,5},{5,4},{6,7},{7,6},{8,9},{9,8},{10,11... | collective-permute-start | bytes 393224 | tf_op jit(solution)/shard_map/ppermute | solution.py:581
  14.7 4.0 %collective-permute-start.5 = (f32[256,128]{1,0:T(8,128)S(1)}, f32[256,128]{1,0:T(8,128)S(1)}, u32[]{:S(2)}, u32[]{:S(2)}) collective-permute-start(f32[256,128]{1,0:T(8,128)S(1)} %collective-permute-done.4.refs_2_), channel_id=1, source_target_pairs={{0,1},{1,0},{2,3},{3,2},{4,5},{5,4},{6,7},{7,6},{8,9},{9,8},{10,11... | collective-permute-start | bytes 393224 | tf_op jit(solution)/shard_map/ppermute | solution.py:581
  16.9 7.3 %collective-permute-start = (f32[8,16,128]{2,1,0:T(8,128)S(1)}, f32[8,16,128]{2,1,0:T(8,128)S(1)}, u32[]{:S(2)}, u32[]{:S(2)}) collective-permute-start(f32[8,16,128]{2,1,0:T(8,128)S(1)} %slice.4.refs_0_), channel_id=1, source_target_pairs={{0,1},{1,0},{2,3},{3,2},{4,5},{5,4},{6,7},{7,6},{8,9},{9,8},{10,11... | collective-permute-start | bytes 196616 | tf_op jit(solution)/shard_map/ppermute | solution.py:581
  16.9 7.3 %collective-permute-start.1 = (f32[8,16,128]{2,1,0:T(8,128)S(1)}, f32[8,16,128]{2,1,0:T(8,128)S(1)}, u32[]{:S(2)}, u32[]{:S(2)}) collective-permute-start(f32[8,16,128]{2,1,0:T(8,128)S(1)} %slice.4.refs_0_), channel_id=1, source_target_pairs={{0,2},{1,3},{2,0},{3,1},{4,6},{5,7},{6,4},{7,5},{8,10},{9,11},{10,... | collective-permute-start | bytes 196616 | tf_op jit(solution)/shard_map/ppermute | solution.py:581
  18.5 5.7 %collective-permute-start.2 = (f32[8,16,128]{2,1,0:T(8,128)S(1)}, f32[8,16,128]{2,1,0:T(8,128)S(1)}, u32[]{:S(2)}, u32[]{:S(2)}) collective-permute-start(f32[8,16,128]{2,1,0:T(8,128)S(1)} %slice.4.refs_0_), channel_id=1, source_target_pairs={{0,3},{1,2},{2,1},{3,0},{4,7},{5,6},{6,5},{7,4},{8,11},{9,10},{10,... | collective-permute-start | bytes 196616 | tf_op jit(solution)/shard_map/ppermute | solution.py:581
  18.8 0.9 %copy-start = (f32[400,128]{1,0:T(8,128)S(1)}, f32[400,128]{1,0:T(8,128)}, u32[]{:S(2)}) copy-start(f32[400,128]{1,0:T(8,128)} %get-tuple-element.17.refs_0_) | copy-start | bytes 614404

commit v6 on v5

--- a/solution.py
+++ b/solution.py
@@ -516,17 +516,21 @@
             direct = pull(now, slot_ref, dist_ref)
             moments, distance = features(ahead, raw_at, ahead_slot), distances(ahead, ahead_dist)
             for step in range(8):
+                early = half == 0 or step < 4
+                run(direct, 1)
+                run(coming, 1)
+                if early:
+                    run(cells, 1)
+                    run(coming, 1)
                 if step % 2 == 1:
                     run(distance, 1)
+                else:
+                    run(moments, 1)
                 run(direct, 1)
-                if step % 2 == 0:
-                    run(moments, 1)
-                if half == 0 or step < 4:
-                    run(coming, 3)
-                    run(cells, 2 if half or step % 2 else 1)
-                else:
+                if early:
                     run(coming, 1)
-                run(direct, 1)
+                    if half or step % 2:
+                        run(cells, 1)
             run(moments)
             run(distance)
             run(direct)

time: 45.5 us -> 46.8 us (1.029)
  Pallas kernels: 27.7 us -> 29.1 us
    pallas_call x1, Pallas kernels: 21 us -> 22.3 us  [on_device(): pl.pallas_call(functools.partial(pull_kernel, n_dom, n_sub), out_shape=ja...]
where the time goes in v6:
time: 46.8 us; the launch traced here: 46.5 us
  Pallas kernels  29.1 us (62%)
  starting transfers between devices  10.6 us (23%)
  waiting for transfers between devices  5.83 us (12%)
  local copies, waits for them, and re-layouts  0.93 us (2%)
    pallas_call x1, Pallas kernels, on_device(): pl.pallas_call(functools.partial(pull_kernel, n_dom, n_sub), out_shape=ja...  22.3 us
    all_to_all x1, starting transfers between devices, on_device(): lax.all_to_all(sent, 'dom', split_axis=0, concat_axis=0, tiled=True)  7.26 us
    pallas_call x1, Pallas kernels, on_device(): pl.pallas_call(functools.partial(prepare_kernel, n_dom, n_sub), out_shape...  4.46 us
    ppermute x6, waiting for transfers between devices, across(): lax.ppermute(value, 'sub', [(seg, seg ^ bits) for seg in range(n_sub)])  3.67 us
    ppermute x6, starting transfers between devices, across(): lax.ppermute(value, 'sub', [(seg, seg ^ bits) for seg in range(n_sub)])  3.38 us
    pallas_call x1, Pallas kernels, on_device(): pl.pallas_call(functools.partial(pack_kernel, n_dom), out_shape=(jax.Shap...  2.29 us
    all_to_all x1, waiting for transfers between devices, on_device(): lax.all_to_all(sent, 'dom', split_axis=0, concat_axis=0, tiled=True)  2.16 us
  transfers between devices with their start and end apart: 7, of which 2 were waited for; matrix products, arithmetic and copies ran while one was open for 0% of the time, Pallas kernels for 10%

profile of v6, /device:TPU:0, one launch (start us, length us, event | category | flops | bytes accessed | tf_op | source)
XLA Modules:
  0.0 46.5 jit_solution(17748040643396905811)
XLA Ops:
  0.0 2.3 %pack_own.1 = (f32[256,128]{1,0:T(8,128)}, f32[8,32,128]{2,1,0:T(8,128)}, f32[400,128]{1,0:T(8,128)}) custom-call(f32[3,8192]{1,0:T(4,128)} %refs_0_.1, f32[1,8192]{1,0:T(1,128)} %bitcast.5, f32[1,128]{1,0:T(1,128)} %bitcast.8, f32[3,128]{1,0:T(4,128)} %refs_3_.1, f32[6,128]{1,0:T(8,128)} %refs_4_.1, s32[128,128]{1,0:T(8,128)} %refs_5_.1, ...), custom_call_target="tpu_custom_call" | custom-call | tf_op jit(solution)/shard_map/pack_own/pallas_call | solution.py:563
  2.3 7.3 %all-to-all-start = ((f32[8,32,128]{2,1,0:T(8,128)}), f32[8,32,128]{2,1,0:T(8,128)S(1)}, u32[]{:S(2)}, u32[]{:S(2)}) async-start(f32[8,32,128]{2,1,0:T(8,128)} %get-tuple-element.16), calls=%async_computation | async-start | bytes 262144 | tf_op jit(solution)/shard_map/all_to_all | solution.py:582
  9.6 1.5 %collective-permute-start.4 = (f32[256,128]{1,0:T(8,128)}, f32[256,128]{1,0:T(8,128)S(1)}, u32[]{:S(2)}, u32[]{:S(2)}) collective-permute-start(f32[256,128]{1,0:T(8,128)} %get-tuple-element.18), channel_id=1, source_target_pairs={{0,2},{1,3},{2,0},{3,1},{4,6},{5,7},{6,4},{7,5},{8,10},{9,11},{10,... | collective-permute-start | bytes 393224 | tf_op jit(solution)/shard_map/ppermute | solution.py:585
  11.1 0.0 collective-permute-start.3
  11.1 3.7 %collective-permute-done.4.refs_2_ = f32[256,128]{1,0:T(8,128)S(1)} collective-permute-done((f32[256,128]{1,0:T(8,128)}, f32[256,128]{1,0:T(8,128)S(1)}, u32[]{:S(2)}, u32[]{:S(2)}) %collective-permute-start.4) | collective-permute-done | bytes 131104 | tf_op jit(solution)/shard_map/ppermute | solution.py:585
  14.7 0.0 collective-permute-start.5
  14.7 2.2 %all-to-all-done.refs_4_ = f32[8,32,128]{2,1,0:T(8,128)S(1)} async-done(((f32[8,32,128]{2,1,0:T(8,128)}), f32[8,32,128]{2,1,0:T(8,128)S(1)}, u32[]{:S(2)}, u32[]{:S(2)}) %all-to-all-start) | async-done | bytes 131104 | tf_op jit(solution)/shard_map/all_to_all | solution.py:582
  16.9 0.0 collective-permute-start
  16.9 1.6 %collective-permute-start.1 = (f32[8,16,128]{2,1,0:T(8,128)S(1)}, f32[8,16,128]{2,1,0:T(8,128)S(1)}, u32[]{:S(2)}, u32[]{:S(2)}) collective-permute-start(f32[8,16,128]{2,1,0:T(8,128)S(1)} %slice.4.refs_0_), channel_id=1, source_target_pairs={{0,2},{1,3},{2,0},{3,1},{4,6},{5,7},{6,4},{7,5},{8,10},{9,11},{10,... | collective-permute-start | bytes 196616 | tf_op jit(solution)/shard_map/ppermute | solution.py:585
  18.5 0.3 collective-permute-start.2
  18.8 0.0 collective-permute-done.3.refs_1_
  18.8 0.0 collective-permute-done.5.refs_3_
  18.8 0.0 copy-start
  18.8 0.9 %copy-done = f32[400,128]{1,0:T(8,128)S(1)} copy-done((f32[400,128]{1,0:T(8,128)S(1)}, f32[400,128]{1,0:T(8,128)}, u32[]{:S(2)}) %copy-start) | copy-done | bytes 204824
  19.7 4.5 %prepare.1 = (f32[576,4,128]{2,1,0:T(4,128)S(1)}, bf16[576,64,128]{2,1,0:T(8,128)(2,1)S(1)}, bf16[64,32,128]{2,1,0:T(8,128)(2,1)S(1)}, f32[256,128]{1,0:T(8,128)...) custom-call(f32[400,128]{1,0:T(8,128)S(1)} %copy-done, ...), custom_call_target="tpu_custom_call" | custom-call | bytes 20000000 | tf_op jit(solution)/shard_map/prepare/pallas_call | solution.py:596
  24.2 0.0 collective-permute-done.refs_1_
  24.2 0.0 collective-permute-done.1.refs_2_
  24.2 0.0 collective-permute-done.2.refs_3_
  24.2 22.3 %pull.1 = f32[3,8192]{1,0:T(4,128)} custom-call(f32[8,16,128]{2,1,0:T(8,128)S(1)} %slice.4.refs_0_, f32[8,16,128]{2,1,0:T(8,128)S(1)} %collective-permute-done.refs_1_, f32[8,16,128]{2,1,0:T(8,128)S(1)} %collective-permute-done.1.refs_2_, f32[8,16,128]{2,1,0:T(8,128)S(1)} %collective-permute-done.2.refs_3_, f32[576,4,128]{2,1,0:T(4,128)S(1)} %get-tuple-element.19.refs_4_, ...), custom_call_target="tpu_custom_call" | custom-call | tf_op jit(solution)/shard_map/pull/pallas_call | solution.py:618
  (1 shorter events, 0.0 us)
Async XLA Ops:
  2.3 14.6 %all-to-all-start = ((f32[8,32,128]{2,1,0:T(8,128)}), f32[8,32,128]{2,1,0:T(8,128)S(1)}, u32[]{:S(2)}, u32[]{:S(2)}) async-start(f32[8,32,128]{2,1,0:T(8,128)} %get-tuple-element.16), calls=%async_computation | async-start | bytes 262144 | tf_op jit(solution)/shard_map/all_to_all | solution.py:582
  9.6 5.2 %collective-permute-start.4 = (f32[256,128]{1,0:T(8,128)}, f32[256,128]{1,0:T(8,128)S(1)}, u32[]{:S(2)}, u32[]{:S(2)}) collective-permute-start(f32[256,128]{1,0:T(8,128)} %get-tuple-element.18), channel_id=1, source_target_pairs={{0,2},{1,3},{2,0},{3,1},{4,6},{5,7},{6,4},{7,5},{8,10},{9,11},{10,... | collective-permute-start | bytes 393224 | tf_op jit(solution)/shard_map/ppermute | solution.py:585
  11.1 7.7 %collective-permute-start.3 = (f32[256,128]{1,0:T(8,128)}, f32[256,128]{1,0:T(8,128)S(1)}, u32[]{:S(2)}, u32[]{:S(2)}) collective-permute-start(f32[256,128]{1,0:T(8,128)} %get-tuple-element.18), channel_id=1, source_target_pairs={{0,1},{1,0},{2,3},{3,2},{4,5},{5,4},{6,7},{7,6},{8,9},{9,8},{10,11... | collective-permute-start | bytes 393224 | tf_op jit(solution)/shard_map/ppermute | solution.py:585
  14.7 4.0 %collective-permute-start.5 = (f32[256,128]{1,0:T(8,128)S(1)}, f32[256,128]{1,0:T(8,128)S(1)}, u32[]{:S(2)}, u32[]{:S(2)}) collective-permute-start(f32[256,128]{1,0:T(8,128)S(1)} %collective-permute-done.4.refs_2_), channel_id=1, source_target_pairs={{0,1},{1,0},{2,3},{3,2},{4,5},{5,4},{6,7},{7,6},{8,9},{9,8},{10,11... | collective-permute-start | bytes 393224 | tf_op jit(solution)/shard_map/ppermute | solution.py:585
  16.9 7.3 %collective-permute-start = (f32[8,16,128]{2,1,0:T(8,128)S(1)}, f32[8,16,128]{2,1,0:T(8,128)S(1)}, u32[]{:S(2)}, u32[]{:S(2)}) collective-permute-start(f32[8,16,128]{2,1,0:T(8,128)S(1)} %slice.4.refs_0_), channel_id=1, source_target_pairs={{0,1},{1,0},{2,3},{3,2},{4,5},{5,4},{6,7},{7,6},{8,9},{9,8},{10,11... | collective-permute-start | bytes 196616 | tf_op jit(solution)/shard_map/ppermute | solution.py:585
  16.9 7.3 %collective-permute-start.1 = (f32[8,16,128]{2,1,0:T(8,128)S(1)}, f32[8,16,128]{2,1,0:T(8,128)S(1)}, u32[]{:S(2)}, u32[]{:S(2)}) collective-permute-start(f32[8,16,128]{2,1,0:T(8,128)S(1)} %slice.4.refs_0_), channel_id=1, source_target_pairs={{0,2},{1,3},{2,0},{3,1},{4,6},{5,7},{6,4},{7,5},{8,10},{9,11},{10,... | collective-permute-start | bytes 196616 | tf_op jit(solution)/shard_map/ppermute | solution.py:585
  18.5 5.7 %collective-permute-start.2 = (f32[8,16,128]{2,1,0:T(8,128)S(1)}, f32[8,16,128]{2,1,0:T(8,128)S(1)}, u32[]{:S(2)}, u32[]{:S(2)}) collective-permute-start(f32[8,16,128]{2,1,0:T(8,128)S(1)} %slice.4.refs_0_), channel_id=1, source_target_pairs={{0,3},{1,2},{2,1},{3,0},{4,7},{5,6},{6,5},{7,4},{8,11},{9,10},{10,... | collective-permute-start | bytes 196616 | tf_op jit(solution)/shard_map/ppermute | solution.py:585
  18.8 0.9 %copy-start = (f32[400,128]{1,0:T(8,128)S(1)}, f32[400,128]{1,0:T(8,128)}, u32[]{:S(2)}) copy-start(f32[400,128]{1,0:T(8,128)} %get-tuple-element.17.refs_0_) | copy-start | bytes 614404

commit v7 on v5

--- a/solution.py
+++ b/solution.py
@@ -522,7 +522,8 @@
                 if step % 2 == 0:
                     run(moments, 1)
                 if half == 0 or step < 4:
-                    run(coming, 3)
+                    if step % 2 == 0:
+                        run(coming, 3 if half and step else 6)
                     run(cells, 2 if half or step % 2 else 1)
                 else:
                     run(coming, 1)

time: 45.5 us -> 45.3 us (level)
  no operation moved by 1% of the time
where the time goes in v7:
time: 45.3 us; the launch traced here: 45 us
  Pallas kernels  27.6 us (61%)
  starting transfers between devices  10.6 us (23%)
  waiting for transfers between devices  5.83 us (13%)
  local copies, waits for them, and re-layouts  0.93 us (2%)
    pallas_call x1, Pallas kernels, on_device(): pl.pallas_call(functools.partial(pull_kernel, n_dom, n_sub), out_shape=ja...  20.8 us
    all_to_all x1, starting transfers between devices, on_device(): lax.all_to_all(sent, 'dom', split_axis=0, concat_axis=0, tiled=True)  7.26 us
    pallas_call x1, Pallas kernels, on_device(): pl.pallas_call(functools.partial(prepare_kernel, n_dom, n_sub), out_shape...  4.46 us
    ppermute x6, waiting for transfers between devices, across(): lax.ppermute(value, 'sub', [(seg, seg ^ bits) for seg in range(n_sub)])  3.67 us
    ppermute x6, starting transfers between devices, across(): lax.ppermute(value, 'sub', [(seg, seg ^ bits) for seg in range(n_sub)])  3.38 us
    pallas_call x1, Pallas kernels, on_device(): pl.pallas_call(functools.partial(pack_kernel, n_dom), out_shape=(jax.Shap...  2.29 us
    all_to_all x1, waiting for transfers between devices, on_device(): lax.all_to_all(sent, 'dom', split_axis=0, concat_axis=0, tiled=True)  2.16 us
    unnamed x2, local copies, waits for them, and re-layouts  0.93 us
  transfers between devices with their start and end apart: 7, of which 2 were waited for; matrix products, arithmetic and copies ran while one was open for 0% of the time, Pallas kernels for 10%

profile of v7, /device:TPU:0, one launch (start us, length us, event | category | flops | bytes accessed | tf_op | source)
XLA Modules:
  0.0 45.0 jit_solution(6659701471862692411)
XLA Ops:
  0.0 2.3 %pack_own.1 = (f32[256,128]{1,0:T(8,128)}, f32[8,32,128]{2,1,0:T(8,128)}, f32[400,128]{1,0:T(8,128)}) custom-call(f32[3,8192]{1,0:T(4,128)} %refs_0_.1, f32[1,8192]{1,0:T(1,128)} %bitcast.5, f32[1,128]{1,0:T(1,128)} %bitcast.8, f32[3,128]{1,0:T(4,128)} %refs_3_.1, f32[6,128]{1,0:T(8,128)} %refs_4_.1, s32[128,128]{1,0:T(8,128)} %refs_5_.1, ...), custom_call_target="tpu_custom_call" | custom-call | tf_op jit(solution)/shard_map/pack_own/pallas_call | solution.py:560
  2.3 7.3 %all-to-all-start = ((f32[8,32,128]{2,1,0:T(8,128)}), f32[8,32,128]{2,1,0:T(8,128)S(1)}, u32[]{:S(2)}, u32[]{:S(2)}) async-start(f32[8,32,128]{2,1,0:T(8,128)} %get-tuple-element.16), calls=%async_computation | async-start | bytes 262144 | tf_op jit(solution)/shard_map/all_to_all | solution.py:579
  9.6 1.5 %collective-permute-start.4 = (f32[256,128]{1,0:T(8,128)}, f32[256,128]{1,0:T(8,128)S(1)}, u32[]{:S(2)}, u32[]{:S(2)}) collective-permute-start(f32[256,128]{1,0:T(8,128)} %get-tuple-element.18), channel_id=1, source_target_pairs={{0,2},{1,3},{2,0},{3,1},{4,6},{5,7},{6,4},{7,5},{8,10},{9,11},{10,... | collective-permute-start | bytes 393224 | tf_op jit(solution)/shard_map/ppermute | solution.py:582
  11.1 0.0 collective-permute-start.3
  11.1 3.7 %collective-permute-done.4.refs_2_ = f32[256,128]{1,0:T(8,128)S(1)} collective-permute-done((f32[256,128]{1,0:T(8,128)}, f32[256,128]{1,0:T(8,128)S(1)}, u32[]{:S(2)}, u32[]{:S(2)}) %collective-permute-start.4) | collective-permute-done | bytes 131104 | tf_op jit(solution)/shard_map/ppermute | solution.py:582
  14.7 0.0 collective-permute-start.5
  14.7 2.2 %all-to-all-done.refs_4_ = f32[8,32,128]{2,1,0:T(8,128)S(1)} async-done(((f32[8,32,128]{2,1,0:T(8,128)}), f32[8,32,128]{2,1,0:T(8,128)S(1)}, u32[]{:S(2)}, u32[]{:S(2)}) %all-to-all-start) | async-done | bytes 131104 | tf_op jit(solution)/shard_map/all_to_all | solution.py:579
  16.9 0.0 collective-permute-start
  16.9 1.6 %collective-permute-start.1 = (f32[8,16,128]{2,1,0:T(8,128)S(1)}, f32[8,16,128]{2,1,0:T(8,128)S(1)}, u32[]{:S(2)}, u32[]{:S(2)}) collective-permute-start(f32[8,16,128]{2,1,0:T(8,128)S(1)} %slice.4.refs_0_), channel_id=1, source_target_pairs={{0,2},{1,3},{2,0},{3,1},{4,6},{5,7},{6,4},{7,5},{8,10},{9,11},{10,... | collective-permute-start | bytes 196616 | tf_op jit(solution)/shard_map/ppermute | solution.py:582
  18.5 0.3 collective-permute-start.2
  18.8 0.0 collective-permute-done.3.refs_1_
  18.8 0.0 collective-permute-done.5.refs_3_
  18.8 0.0 copy-start
  18.8 0.9 %copy-done = f32[400,128]{1,0:T(8,128)S(1)} copy-done((f32[400,128]{1,0:T(8,128)S(1)}, f32[400,128]{1,0:T(8,128)}, u32[]{:S(2)}) %copy-start) | copy-done | bytes 204824
  19.7 4.5 %prepare.1 = (f32[576,4,128]{2,1,0:T(4,128)S(1)}, bf16[576,64,128]{2,1,0:T(8,128)(2,1)S(1)}, bf16[64,32,128]{2,1,0:T(8,128)(2,1)S(1)}, f32[256,128]{1,0:T(8,128)...) custom-call(f32[400,128]{1,0:T(8,128)S(1)} %copy-done, ...), custom_call_target="tpu_custom_call" | custom-call | bytes 20000000 | tf_op jit(solution)/shard_map/prepare/pallas_call | solution.py:593
  24.2 0.0 collective-permute-done.refs_1_
  24.2 0.0 collective-permute-done.1.refs_2_
  24.2 0.0 collective-permute-done.2.refs_3_
  24.2 20.8 %pull.1 = f32[3,8192]{1,0:T(4,128)} custom-call(f32[8,16,128]{2,1,0:T(8,128)S(1)} %slice.4.refs_0_, f32[8,16,128]{2,1,0:T(8,128)S(1)} %collective-permute-done.refs_1_, f32[8,16,128]{2,1,0:T(8,128)S(1)} %collective-permute-done.1.refs_2_, f32[8,16,128]{2,1,0:T(8,128)S(1)} %collective-permute-done.2.refs_3_, f32[576,4,128]{2,1,0:T(4,128)S(1)} %get-tuple-element.19.refs_4_, ...), custom_call_target="tpu_custom_call" | custom-call | tf_op jit(solution)/shard_map/pull/pallas_call | solution.py:615
  (1 shorter events, 0.0 us)
Async XLA Ops:
  2.3 14.6 %all-to-all-start = ((f32[8,32,128]{2,1,0:T(8,128)}), f32[8,32,128]{2,1,0:T(8,128)S(1)}, u32[]{:S(2)}, u32[]{:S(2)}) async-start(f32[8,32,128]{2,1,0:T(8,128)} %get-tuple-element.16), calls=%async_computation | async-start | bytes 262144 | tf_op jit(solution)/shard_map/all_to_all | solution.py:579
  9.6 5.2 %collective-permute-start.4 = (f32[256,128]{1,0:T(8,128)}, f32[256,128]{1,0:T(8,128)S(1)}, u32[]{:S(2)}, u32[]{:S(2)}) collective-permute-start(f32[256,128]{1,0:T(8,128)} %get-tuple-element.18), channel_id=1, source_target_pairs={{0,2},{1,3},{2,0},{3,1},{4,6},{5,7},{6,4},{7,5},{8,10},{9,11},{10,... | collective-permute-start | bytes 393224 | tf_op jit(solution)/shard_map/ppermute | solution.py:582
  11.1 7.7 %collective-permute-start.3 = (f32[256,128]{1,0:T(8,128)}, f32[256,128]{1,0:T(8,128)S(1)}, u32[]{:S(2)}, u32[]{:S(2)}) collective-permute-start(f32[256,128]{1,0:T(8,128)} %get-tuple-element.18), channel_id=1, source_target_pairs={{0,1},{1,0},{2,3},{3,2},{4,5},{5,4},{6,7},{7,6},{8,9},{9,8},{10,11... | collective-permute-start | bytes 393224 | tf_op jit(solution)/shard_map/ppermute | solution.py:582
  14.7 4.0 %collective-permute-start.5 = (f32[256,128]{1,0:T(8,128)S(1)}, f32[256,128]{1,0:T(8,128)S(1)}, u32[]{:S(2)}, u32[]{:S(2)}) collective-permute-start(f32[256,128]{1,0:T(8,128)S(1)} %collective-permute-done.4.refs_2_), channel_id=1, source_target_pairs={{0,1},{1,0},{2,3},{3,2},{4,5},{5,4},{6,7},{7,6},{8,9},{9,8},{10,11... | collective-permute-start | bytes 393224 | tf_op jit(solution)/shard_map/ppermute | solution.py:582
  16.9 7.3 %collective-permute-start = (f32[8,16,128]{2,1,0:T(8,128)S(1)}, f32[8,16,128]{2,1,0:T(8,128)S(1)}, u32[]{:S(2)}, u32[]{:S(2)}) collective-permute-start(f32[8,16,128]{2,1,0:T(8,128)S(1)} %slice.4.refs_0_), channel_id=1, source_target_pairs={{0,1},{1,0},{2,3},{3,2},{4,5},{5,4},{6,7},{7,6},{8,9},{9,8},{10,11... | collective-permute-start | bytes 196616 | tf_op jit(solution)/shard_map/ppermute | solution.py:582
  16.9 7.3 %collective-permute-start.1 = (f32[8,16,128]{2,1,0:T(8,128)S(1)}, f32[8,16,128]{2,1,0:T(8,128)S(1)}, u32[]{:S(2)}, u32[]{:S(2)}) collective-permute-start(f32[8,16,128]{2,1,0:T(8,128)S(1)} %slice.4.refs_0_), channel_id=1, source_target_pairs={{0,2},{1,3},{2,0},{3,1},{4,6},{5,7},{6,4},{7,5},{8,10},{9,11},{10,... | collective-permute-start | bytes 196616 | tf_op jit(solution)/shard_map/ppermute | solution.py:582
  18.5 5.7 %collective-permute-start.2 = (f32[8,16,128]{2,1,0:T(8,128)S(1)}, f32[8,16,128]{2,1,0:T(8,128)S(1)}, u32[]{:S(2)}, u32[]{:S(2)}) collective-permute-start(f32[8,16,128]{2,1,0:T(8,128)S(1)} %slice.4.refs_0_), channel_id=1, source_target_pairs={{0,3},{1,2},{2,1},{3,0},{4,7},{5,6},{6,5},{7,4},{8,11},{9,10},{10,... | collective-permute-start | bytes 196616 | tf_op jit(solution)/shard_map/ppermute | solution.py:582
  18.8 0.9 %copy-start = (f32[400,128]{1,0:T(8,128)S(1)}, f32[400,128]{1,0:T(8,128)}, u32[]{:S(2)}) copy-start(f32[400,128]{1,0:T(8,128)} %get-tuple-element.17.refs_0_) | copy-start | bytes 614404
